TPU v7x, 32 devices: a whole 2x2x4 slice. The times are simulated.
32 devices in a mesh: batch: 2 (over y), seq: 16 (over z, x, core).
Axes of the slice: x: 2, y: 2, z: 4, core: 2. Of those that a mesh axis runs over, the one named last changes fastest.
Arguments:
- tokens_in: bfloat16 [4, 4096, 768], P('batch', 'seq'), may hold values from -6 to 6
- earlier_outs: bfloat16 [9, 4, 4096, 768], P(None, 'batch', 'seq'), may hold values from -6 to 6
- out_cotangent: bfloat16 [4, 4096, 768], P('batch', 'seq'), may hold values from -6 to 6
- seq_lengths: int32 [4], P('batch'), may hold values from 1 to 4096, as said below
- qkv_weight: float32 [768, 2304], P(('batch', 'seq')), may hold values from -0.21875 to 0.21875
- out_weight: float32 [768, 768], P(('batch', 'seq')), may hold values from -1.75 to 1.75
- up_weight: float32 [768, 3072], P(('batch', 'seq')), may hold values from -0.21875 to 0.21875
- down_weight: float32 [3072, 768], P(('batch', 'seq')), may hold values from -0.109375 to 0.109375
- qkv_first: float32 [768, 2304], P(('batch', 'seq')), may hold values from -60 to 60
- qkv_second: float32 [768, 2304], P(('batch', 'seq')), may hold values from 1 to 10000
- out_first: float32 [768, 768], P(('batch', 'seq')), may hold values from -60 to 60
- out_second: float32 [768, 768], P(('batch', 'seq')), may hold values from 1 to 10000
- up_first: float32 [768, 3072], P(('batch', 'seq')), may hold values from -60 to 60
- up_second: float32 [768, 3072], P(('batch', 'seq')), may hold values from 1 to 10000
- down_first: float32 [3072, 768], P(('batch', 'seq')), may hold values from -60 to 60
- down_second: float32 [3072, 768], P(('batch', 'seq')), may hold values from 1 to 10000
- small_params: float32 [9995], replicated, may hold values from -1.5 to 1.5
- small_first: float32 [9995], replicated, may hold values from -60 to 60
- small_second: float32 [9995], replicated, may hold values from 1 to 10000
Outputs:
- mixed: bfloat16 [4, 4096, 768], P('batch', 'seq')
- input_grad: float32 [4, 4096, 768], P('batch', 'seq')
- qkv_grad: float32 [768, 2304], P(('batch', 'seq'))
- out_grad: float32 [768, 768], P(('batch', 'seq'))
- up_grad: float32 [768, 3072], P(('batch', 'seq'))
- down_grad: float32 [3072, 768], P(('batch', 'seq'))
- small_grad: float32 [9995], replicated
- qkv_step: float32 [768, 2304], P(('batch', 'seq'))
- out_step: float32 [768, 768], P(('batch', 'seq'))
- up_step: float32 [768, 3072], P(('batch', 'seq'))
- down_step: float32 [3072, 768], P(('batch', 'seq'))
- small_step: float32 [9995], replicated
- qkv_first_new: float32 [768, 2304], P(('batch', 'seq'))
- out_first_new: float32 [768, 768], P(('batch', 'seq'))
- up_first_new: float32 [768, 3072], P(('batch', 'seq'))
- down_first_new: float32 [3072, 768], P(('batch', 'seq'))
- small_first_new: float32 [9995], replicated
Inputs may be any that keep to these rules, and one draw needn't show every extreme that they name: `seq_lengths`: in every group of 2 consecutive slots (the sequences of one batch index) one slot has length 4096.
All inputs are finite; a program needn't handle non-finite values.
Results may differ from a plain program's by a relative error of at most 0.015.
Values may be sent and summed in bfloat16 or wider, within the bound.
A program may use at most 128 MiB of HBM per device.

v0:
```python
import functools
import math

import jax
import jax.numpy as jnp
from jax import lax
from jax.experimental import pallas as pl
from jax.experimental.pallas import tpu as pltpu
from jax.sharding import PartitionSpec as P

D = 768
FF = 3072
HEAD = 64
BLOCKS = FF // D
VECTORS = 9 + BLOCKS
bf16 = jnp.bfloat16
f32 = jnp.float32
NEG = -1e30

beta_one = 0.9
beta_two = 0.999
adam_eps = 1e-08
learn_rate = 0.01
decay_rate = 0.1
adam_step = 10

MESH = pl.DeviceIdType.MESH
ANYWHERE = pl.BlockSpec(memory_space=pl.ANY)
IN_VMEM = pl.BlockSpec(memory_space=pltpu.VMEM)
IN_SMEM = pl.BlockSpec(memory_space=pltpu.SMEM)
DMA = pltpu.SemaphoreType.DMA
ROOM = 56 << 20

UNITS = ((0, 1, 4), (2, 3, 5))


def mm(a, b):
    return lax.dot_general(a, b, (((1,), (0,)), ((), ())), preferred_element_type=f32)


def mm_nt(a, b):
    return lax.dot_general(a, b, (((1,), (1,)), ((), ())), preferred_element_type=f32)


def params():
    return pltpu.CompilerParams(vmem_limit_bytes=ROOM)


def remote_params(ident, vmem=None):
    return pltpu.CompilerParams(collective_id=ident, has_side_effects=True, vmem_limit_bytes=vmem)


class Place:
    def __init__(self, batches, outer, inner):
        self.batch = lax.axis_index("batch")
        rank = lax.axis_index("seq")
        self.o = lax.div(rank, inner)
        self.j = lax.rem(rank, inner)
        self.a = lax.div(self.j, 2)
        self.c = lax.rem(rank, 2)
        across = inner // 2
        self.zs = [lax.rem(self.o + t, outer) for t in range(outer)]
        self.xs = [lax.rem(self.a + t, across) for t in range(across)]
        self.ys = [lax.rem(self.batch + t, batches) for t in range(batches)]
        self.z_from = [lax.rem(self.o + outer - t, outer) for t in range(outer)]
        self.x_from = [lax.rem(self.a + across - t, across) for t in range(across)]
        self.y_from = [lax.rem(self.batch + batches - t, batches) for t in range(batches)]
        self.z_peers = [(self.batch, z * inner + self.j) for z in self.zs]
        self.x_peers = [(self.batch, self.o * inner + x * 2 + self.c) for x in self.xs]
        self.y_peers = [(y, rank) for y in self.ys]
        self.twin = (self.batch, self.o * inner + self.a * 2 + (1 - self.c))


def greet(peers):
    barrier = pltpu.get_barrier_semaphore()
    for peer in peers:
        pl.semaphore_signal(barrier, inc=1, device_id=peer, device_id_type=MESH)
    pl.semaphore_wait(barrier, len(peers))


def push(src, dst, send, recv, peer):
    copy = pltpu.make_async_remote_copy(
        src_ref=src, dst_ref=dst, send_sem=send, recv_sem=recv, device_id=peer, device_id_type=MESH
    )
    copy.start()
    return copy


def carry(src, dst, sem):
    copy = pltpu.make_async_copy(src, dst, sem)
    copy.start()
    return copy


def normalize(values):
    center = values - jnp.mean(values, -1, keepdims=True)
    inverse = lax.rsqrt(jnp.mean(center * center, -1, keepdims=True) + 1e-05)
    return center * inverse, inverse


def normalize_back(grad, hat, inverse, gain):
    scaled = grad * gain
    part = scaled - jnp.mean(scaled, -1, keepdims=True) - hat * jnp.mean(scaled * hat, -1, keepdims=True)
    return part * inverse


def turn(value, cosine, sine):
    lane = lax.broadcasted_iota(jnp.int32, value.shape, 1)
    other = jnp.where(lax.rem(lane, HEAD) < HEAD // 2, pltpu.roll(value, 128 - HEAD // 2, 1), pltpu.roll(value, HEAD // 2, 1))
    return value * cosine + other * sine


def put_heads(write, tiles_of, outer):
    for o in range(outer):
        first = 3 * o * HEAD
        odd = first % 128 != 0
        pair = (first + HEAD if odd else first) // 128
        single = (first if odd else first + 128) // 128
        write(o, 0, tiles_of(0, pair))
        write(o, 1, tiles_of(1, pair))
        one, two = tiles_of(0, single), tiles_of(1, single)
        if odd:
            one = pltpu.roll(one, HEAD, 1)
        else:
            two = pltpu.roll(two, HEAD, 1)
        lane = lax.broadcasted_iota(jnp.int32, one.shape, 1)
        write(o, 2, jnp.where(lane < HEAD, one, two))


def take_heads(read, g, outer):
    tiles = [None] * (outer * 3 // 2)
    for o in range(0, outer, 2):
        base = 3 * o * HEAD // 128
        tiles[base] = read(o, g)
        tiles[base + 2] = read(o + 1, g)
        low, high = read(o, 2), read(o + 1, 2)
        if g == 0:
            high = pltpu.roll(high, HEAD, 1)
        else:
            low = pltpu.roll(low, HEAD, 1)
        lane = lax.broadcasted_iota(jnp.int32, low.shape, 1)
        tiles[base + 1] = jnp.where(lane < HEAD, low, high)
    return tiles


def first_kernel(batches, outer, inner, first_row, *refs):
    refs = list(refs)

    def take(n):
        got = refs[:n]
        del refs[:n]
        return got

    qkv, out, up, down, lens, mixing, tokens, cot, earlier, vecs, count = take(11)
    near_all, up_line, down_line, counts, normed, mixture, dots = take(7)
    own, got, near, up_bit, down_bit, queue = take(6)
    zs, zr, xs, xr, ys, yr, cs, cr, us, ur, ds, dr, ns, nr, ts, tr, local, es = refs
    across = inner // 2
    here = Place(batches, outer, inner)
    o, a, b, c = here.o, here.a, here.batch, here.c
    earlier_count, tall, _ = earlier.shape
    groups = lens.shape[0]
    rows = tall // groups
    fetches = {}
    for e in range(2):
        fetches[e] = carry(earlier.at[e], queue.at[e], es.at[e])
    for block in range(4):
        own[block] = qkv[:, block * D : block * D + D] if block < 3 else out[...]
        own[4 + block] = up[:, block * D : block * D + D]
    greet(here.z_peers[1:] + here.x_peers[1:] + here.y_peers[1:] + [here.twin])
    theirs = 2 * (1 - c)
    swaps = [
        push(own.at[pl.ds(theirs, 2)], got.at[0], ts.at[0], tr.at[0], here.twin),
        push(own.at[pl.ds(4 + theirs, 2)], got.at[1], ts.at[1], tr.at[1], here.twin),
    ]
    waits = [carry(count, counts.at[b], local.at[0])]
    for d in range(1, batches):
        waits.append(push(count, counts.at[b], ns.at[d], nr.at[d], here.y_peers[d]))
    down_bit[...] = down[...].astype(bf16)

    def joined(kind, p):
        mine, other = own[4 * kind + 2 * c + p], got[kind, p]
        low = jnp.where(c == 0, mine, other)
        high = jnp.where(c == 0, other, mine)
        return jnp.concatenate([low, high], 0).astype(bf16)

    def slot(p, y, z, x):
        return near_all.at[2 * c + p, y, z, x]

    arrivals = {}

    def onward(source, p, y, z, x, t, dx, dy):
        to = slot(p, y, z, x)
        if dx == 0 and (dy == 0 or p == 1):
            for d in range(1, across):
                key = (p, t, d, dy)
                arrivals["x", key] = push(source, to, xs.at[key], xr.at[key], here.x_peers[d])
        if dy == 0 and (dx == 0 or p == 0):
            for d in range(1, batches):
                key = (p, t, dx, d)
                arrivals["y", key] = push(source, to, ys.at[key], yr.at[key], here.y_peers[d])
        key = (p, t, dx, dy)
        waits.append(push(source, to, cs.at[key], cr.at[key], here.twin))

    swaps[0].wait()
    copies = {}
    for p in (0, 1):
        near[p] = joined(0, p)
        for t in range(1, outer):
            copies[t, p] = push(near.at[p], slot(p, b, o, a), zs.at[t, p], zr.at[t, p], here.z_peers[t])
        onward(near.at[p], p, b, o, a, 0, 0, 0)
        waits.append(carry(near.at[p], slot(p, b, o, a), local.at[1 + p]))
    swaps[1].wait()
    for p in (0, 1):
        up_bit[p] = joined(1, p)
    for t in range(1, outer):
        waits.append(push(up_bit, up_line.at[:, o], us.at[t], ur.at[t], here.z_peers[t]))
        waits.append(push(down_bit, down_line.at[o], ds.at[t], dr.at[t], here.z_peers[t]))
    waits.append(carry(up_bit, up_line.at[:, o], local.at[3]))
    waits.append(carry(down_bit, down_line.at[o], local.at[4]))

    def live_rows(value):
        row = lax.broadcasted_iota(jnp.int32, (rows, 1), 0) + first_row(rows)
        parts = [jnp.where(row < lens[g], value[g * rows : g * rows + rows], 0.0) for g in range(groups)]
        return jnp.concatenate(parts, 0)

    def normal():
        wide = tokens[...].astype(f32)
        hat, _ = normalize(wide)
        normed[...] = (hat * vecs[0:1] + vecs[2:3]).astype(bf16)
        grad = live_rows(cot[...].astype(f32))
        dots[...] = jnp.zeros(dots.shape, f32)
        dots[1:2] = jnp.sum(grad * wide, 0, keepdims=True)
        mixture[...] = mixing[1] * wide

    def mix(e):
        fetches[e].wait()
        wide = queue[e % 2].astype(f32)
        grad = live_rows(cot[...].astype(f32))
        dots[2 + e : 3 + e] = jnp.sum(grad * wide, 0, keepdims=True)
        mixture[...] = mixture[...] + mixing[2 + e] * wide
        if e + 2 < earlier_count:
            fetches[e + 2] = carry(earlier.at[e + 2], queue.at[e % 2], es.at[e + 2])

    steps = [normal] + [functools.partial(mix, e) for e in range(earlier_count)]

    def work(n=1):
        for _ in range(n):
            if steps:
                steps.pop(0)()

    for t in range(1, outer):
        for p in (0, 1):
            copies[t, p].wait()
            onward(slot(p, b, here.z_from[t], a), p, b, here.z_from[t], a, t, 0, 0)
    work(1)
    for t in range(outer):
        z = here.z_from[t]
        for d in range(1, across):
            arrivals["x", (0, t, d, 0)].wait()
            onward(slot(0, b, z, here.x_from[d]), 0, b, z, here.x_from[d], t, d, 0)
        for d in range(1, batches):
            arrivals["y", (1, t, 0, d)].wait()
            onward(slot(1, here.y_from[d], z, a), 1, here.y_from[d], z, a, t, 0, d)
        work(1)
    for t in range(outer):
        z = here.z_from[t]
        for dx in range(across):
            for dy in range(1, batches):
                arrivals["y", (0, t, dx, dy)].wait()
                onward(slot(0, here.y_from[dy], z, here.x_from[dx]), 0, here.y_from[dy], z, here.x_from[dx], t, dx, dy)
        for dy in range(batches):
            for dx in range(1, across):
                arrivals["x", (1, t, dx, dy)].wait()
                onward(slot(1, here.y_from[dy], z, here.x_from[dx]), 1, here.y_from[dy], z, here.x_from[dx], t, dx, dy)
        work(1)
    work(len(steps))
    for copy in waits:
        copy.wait()


def gather_first(qkv, out, up, down, lens, mixing, tokens, cot, earlier, vecs, count, batches, outer, inner, ident):
    across = inner // 2
    share = qkv.shape[0]
    tall = tokens.shape[0]

    def first_row(rows):
        return lax.axis_index("seq") * rows

    grid = (batches, outer, across)
    return pl.pallas_call(
        functools.partial(first_kernel, batches, outer, inner, first_row),
        out_shape=(
            jax.ShapeDtypeStruct((4,) + grid + (2 * share, D), bf16),
            jax.ShapeDtypeStruct((2, outer, 2 * share, D), bf16),
            jax.ShapeDtypeStruct((outer, BLOCKS * share, D), bf16),
            jax.ShapeDtypeStruct((batches,) + count.shape, count.dtype),
            jax.ShapeDtypeStruct((tall, D), bf16),
            jax.ShapeDtypeStruct((tall, D), f32),
            jax.ShapeDtypeStruct((16, D), f32),
        ),
        in_specs=[IN_VMEM] * 4 + [IN_SMEM] * 2 + [IN_VMEM] * 2 + [ANYWHERE, IN_VMEM, ANYWHERE],
        out_specs=(ANYWHERE,) * 4 + (IN_VMEM,) * 3,
        scratch_shapes=[
            pltpu.VMEM((8, share, D), f32),
            pltpu.VMEM((2, 2, share, D), f32),
            pltpu.VMEM((2, 2 * share, D), bf16),
            pltpu.VMEM((2, 2 * share, D), bf16),
            pltpu.VMEM((BLOCKS * share, D), bf16),
            pltpu.VMEM((2, tall, D), bf16),
        ]
        + [DMA((outer, 2))] * 2
        + [DMA((2, outer, across, batches))] * 6
        + [DMA((outer,))] * 4
        + [DMA((batches,))] * 2
        + [DMA((2,))] * 2
        + [DMA((5,)), DMA((earlier.shape[0],))],
        compiler_params=remote_params(ident, ROOM),
        name="gather_first",
    )(qkv, out, up, down, lens, mixing, tokens, cot, earlier, vecs, count)


def spread_kernel(batches, outer, inner, with_rest, *refs):
    refs = list(refs)

    def take(n):
        got = refs[:n]
        del refs[:n]
        return got

    normed, near, vecs, cosine, sine = take(5)
    lines = take(2) if with_rest else []
    q_all, k_all, v_all = take(3)
    alls = take(2) if with_rest else []
    q, k, v, work = take(4)
    qs, qr, zs, zr, xs, xr, cs, cr, local = take(9)
    across = inner // 2
    here = Place(batches, outer, inner)
    o, a, b, c, j = here.o, here.a, here.batch, here.c, here.j
    rows = cosine.shape[0]
    greet(here.z_peers[1:] + here.x_peers[1:] + [here.twin] + (here.y_peers[1:] if with_rest else []))
    waits, rest_x, rest_y = [], [], []

    def rest_slot(i, y, x):
        if i == 0:
            return alls[0].at[pl.ds(2 * c, 2), y, :, x]
        return alls[1].at[y, :, x, c]

    if with_rest:
        ax, axr, ay, ayr, ac, acr, alocal = refs
        for i in (0, 1):
            waits.append(carry(lines[i], rest_slot(i, b, a), alocal.at[i]))
            for d in range(1, across):
                rest_x.append((i, d, push(lines[i], rest_slot(i, b, a), ax.at[i, d], axr.at[i, d], here.x_peers[d])))
            for d in range(1, batches):
                rest_y.append((i, 0, d, push(lines[i], rest_slot(i, b, a), ay.at[i, 0, d], ayr.at[i, 0, d], here.y_peers[d])))
            waits.append(push(lines[i], rest_slot(i, b, a), ac.at[i, 0, 0], acr.at[i, 0, 0], here.twin))

    def rest_across():
        i, d, copy = rest_x.pop(0)
        copy.wait()
        piece = rest_slot(i, b, here.x_from[d])
        for e in range(1, batches):
            rest_y.append((i, d, e, push(piece, piece, ay.at[i, d, e], ayr.at[i, d, e], here.y_peers[e])))
        waits.append(push(piece, piece, ac.at[i, d, 0], acr.at[i, d, 0], here.twin))

    def rest_twin():
        i, d, e, copy = rest_y.pop(0)
        copy.wait()
        piece = rest_slot(i, here.y_from[e], here.x_from[d])
        waits.append(push(piece, piece, ac.at[i, d, e], acr.at[i, d, e], here.twin))

    def project(block, into, rotated):
        work[...] = mm(normed[...], near[block]) + vecs[4 + block : 5 + block]

        def tiles_of(g, tile):
            value = work[g * rows : g * rows + rows, 128 * tile : 128 * tile + 128]
            return turn(value, cosine[...], sine[...]) if rotated else value

        def write(target, tile, value):
            into[target, :, 128 * tile : 128 * tile + 128] = value.astype(bf16)

        put_heads(write, tiles_of, outer)

    arriving, own = [], []
    for i, (block, into, dest) in enumerate(((1, k, k_all), (2, v, v_all))):
        project(block, into, i == 0)
        for t in range(1, outer):
            copy = push(into.at[here.zs[t]], dest.at[o, j], zs.at[i, t], zr.at[i, t], here.z_peers[t])
            arriving.append((i, t, copy))
        waits.append(carry(into.at[o], dest.at[o, j], local.at[i]))
        own.append((i, 0, None))
    project(0, q, True)
    for t in range(1, outer):
        waits.append(push(q.at[here.zs[t]], q_all.at[o], qs.at[t], qr.at[t], here.z_peers[t]))
    waits.append(carry(q.at[o], q_all.at[o], local.at[2]))
    late = []
    order = own + arriving
    for n, (i, t, copy) in enumerate(order):
        dest = (k_all, v_all)[i]
        place = dest.at[here.z_from[t], j]
        source = (k, v)[i].at[o] if copy is None else place
        if copy is not None:
            copy.wait()
        for d in range(1, across):
            late.append((i, t, d, push(source, place, xs.at[i, t, d], xr.at[i, t, d], here.x_peers[d])))
        waits.append(push(source, place, cs.at[i, t, 0], cr.at[i, t, 0], here.twin))
        while len(late) > (across - 1 if n < len(order) - 1 else 0):
            li, lt, ld, waited = late.pop(0)
            waited.wait()
            moved = (k_all, v_all)[li].at[here.z_from[lt], here.x_from[ld] * 2 + c]
            waits.append(push(moved, moved, cs.at[li, lt, ld], cr.at[li, lt, ld], here.twin))
        if rest_x and n >= 2:
            rest_across()
    while rest_x:
        rest_across()
    while rest_y:
        rest_twin()
    for copy in waits:
        copy.wait()


def spread_heads(normed, near, vecs, cosine, sine, lines, batches, outer, inner, ident):
    rows = cosine.shape[0]
    across = inner // 2
    width = 2 * D // outer
    with_rest = bool(lines)
    piece = jax.ShapeDtypeStruct((outer, rows, width), bf16)
    full = jax.ShapeDtypeStruct((outer, inner, rows, width), bf16)
    shapes = (piece, full, full)
    scratch = [pltpu.VMEM((outer, rows, width), bf16)] * 3 + [pltpu.VMEM(normed.shape, f32)]
    scratch += [DMA((outer,))] * 2 + [DMA((2, outer))] * 2 + [DMA((2, outer, across))] * 4 + [DMA((3,))]
    if with_rest:
        shapes += (
            jax.ShapeDtypeStruct((4, batches, outer, across) + lines[0].shape[2:], bf16),
            jax.ShapeDtypeStruct((batches, outer, across, 2) + lines[1].shape[1:], bf16),
        )
        scratch += [DMA((2, across))] * 2 + [DMA((2, across, batches))] * 4 + [DMA((2,))]
    return pl.pallas_call(
        functools.partial(spread_kernel, batches, outer, inner, with_rest),
        out_shape=shapes,
        in_specs=[IN_VMEM] * 5 + [ANYWHERE] * len(lines),
        out_specs=(ANYWHERE,) * len(shapes),
        scratch_shapes=scratch,
        compiler_params=remote_params(ident, ROOM),
        name="spread_heads",
    )(normed, near, vecs, cosine, sine, *lines)


def swap_kernel(batches, inner, x, out, send, recv, local):
    outer = x.shape[0]
    here = Place(batches, outer, inner)
    greet(here.z_peers[1:])
    own = carry(x.at[here.o], out.at[here.o], local)
    copies = []
    for t in range(1, outer):
        copies.append(push(x.at[here.zs[t]], out.at[here.o], send.at[t], recv.at[t], here.z_peers[t]))
    own.wait()
    for copy in copies:
        copy.wait()


def swap_outer(x, batches, inner, ident):
    outer = x.shape[0]
    return pl.pallas_call(
        functools.partial(swap_kernel, batches, inner),
        out_shape=jax.ShapeDtypeStruct(x.shape, x.dtype),
        in_specs=[ANYWHERE],
        out_specs=ANYWHERE,
        scratch_shapes=[DMA((outer,)), DMA((outer,)), DMA],
        compiler_params=remote_params(ident),
        name="swap_heads",
    )(x)


def half_rows(block_t, half):
    z = jnp.zeros((HEAD, block_t.shape[1]), block_t.dtype)
    if half == 0:
        return jnp.concatenate([block_t[:HEAD], z], 0)
    return jnp.concatenate([z, block_t[HEAD:]], 0)


def attend_kernel(groups, per, span, inner, lens, q, k, v, o, ot, lse, vt, qt, m_s, l_s):
    outer, rows, width = q.shape
    units = groups * per
    total = k.shape[0]
    j = lax.rem(lax.axis_index("seq"), inner)
    blk = math.gcd(total, 512)

    def turn_v(i, _):
        at = pl.ds(pl.multiple_of(i * blk, blk), blk)
        for t in range(width // 128):
            lanes = slice(128 * t, 128 * t + 128)
            vt[lanes, at] = v[at, lanes].T
        return 0

    lax.fori_loop(0, total // blk, turn_v, 0)

    def one(z, _):
        first = (z * inner + j) * rows
        for t in range(width // 128):
            lanes = slice(128 * t, 128 * t + 128)
            turned = (q[z, :, lanes] * 0.125).astype(bf16).T
            for half in range(2):
                qt[2 * t + half] = half_rows(turned, half)
        for g in range(groups):
            length = lens[g]
            for u in UNITS[g]:
                ot[z, HEAD * u : HEAD * u + HEAD, :] = jnp.zeros((HEAD, rows), f32)
            m_s[...] = jnp.full(m_s.shape, NEG, f32)
            l_s[...] = jnp.zeros(l_s.shape, f32)

            def step(c, masked):
                at = pl.ds(pl.multiple_of(c * span, span), span)
                if masked:
                    key = c * span + lax.broadcasted_iota(jnp.int32, (span, rows), 0)
                    query = first + lax.broadcasted_iota(jnp.int32, (span, rows), 1)
                    allowed = (key <= query) & (key < length)
                scores, tops, news, shares, sums = [], [], [], [], []
                for h in range(per):
                    u = UNITS[g][h]
                    s = mm(k[at, 128 * (u // 2) : 128 * (u // 2) + 128], qt[u])
                    scores.append(jnp.where(allowed, s, NEG) if masked else s)
                for h in range(per):
                    tops.append(m_s[h : h + 1])
                    news.append(jnp.maximum(tops[h], jnp.max(scores[h], 0, keepdims=True)))
                for h in range(per):
                    p = jnp.exp(scores[h] - news[h])
                    sums.append(jnp.sum(p, 0, keepdims=True))
                    shares.append(p.astype(bf16))
                for h in range(per):
                    u = UNITS[g][h]
                    alpha = jnp.exp(tops[h] - news[h])
                    l_s[h : h + 1] = l_s[h : h + 1] * alpha + sums[h]
                    m_s[h : h + 1] = news[h]
                    span_u = slice(HEAD * u, HEAD * u + HEAD)
                    ot[z, span_u, :] = ot[z, span_u, :] * alpha + mm(vt[span_u, at], shares[h])

            whole = jnp.minimum(first, length) // span
            count = (jnp.minimum(first + rows, length) + span - 1) // span

            def full_step(c, _):
                step(c, False)
                return 0

            def edge_step(c, _):
                step(c, True)
                return 0

            lax.fori_loop(0, whole, full_step, 0)
            lax.fori_loop(whole, count, edge_step, 0)
            for h in range(per):
                u = UNITS[g][h]
                span_u = slice(HEAD * u, HEAD * u + HEAD)
                total_exp = l_s[h : h + 1]
                ot[z, span_u, :] = ot[z, span_u, :] / total_exp
                lse[z, u : u + 1, :] = m_s[h : h + 1] + jnp.log(total_exp)
        for t in range(width // 128):
            lanes = slice(128 * t, 128 * t + 128)
            o[z, :, lanes] = ot[z, lanes, :].T.astype(bf16)
        return 0

    lax.fori_loop(0, outer, one, 0)


def attend(lens, q, k, v, groups, per, inner, span):
    outer, rows, width = q.shape
    units = groups * per
    total = k.shape[0]
    vm = IN_VMEM
    return pl.pallas_call(
        functools.partial(attend_kernel, groups, per, span, inner),
        out_shape=(
            jax.ShapeDtypeStruct((outer, rows, width), bf16),
            jax.ShapeDtypeStruct((outer, width, rows), f32),
            jax.ShapeDtypeStruct((outer, 8, rows), f32),
        ),
        in_specs=[IN_SMEM, vm, vm, vm],
        out_specs=(vm, vm, vm),
        scratch_shapes=[
            pltpu.VMEM((width, total), bf16),
            pltpu.VMEM((units, 128, rows), bf16),
            pltpu.VMEM((8, rows), f32),
            pltpu.VMEM((8, rows), f32),
        ],
        compiler_params=params(),
        name="attend",
    )(lens, q, k, v)


def attend_back_kernel(groups, per, span, inner, lens, q, k, v, do, ot, lse, cos, sin, dq, dk, dv, kt, qt, dot_t, qz, dz, rd, dqt, dks, dvs):
    outer, rows, width = q.shape
    units = groups * per
    total = k.shape[0]
    j = lax.rem(lax.axis_index("seq"), inner)
    blk = math.gcd(total, 512)

    def prepare(i, _):
        at = pl.ds(pl.multiple_of(i * blk, blk), blk)
        for t in range(width // 128):
            lanes = slice(128 * t, 128 * t + 128)
            kt[lanes, at] = k[at, lanes].T
        dks[at, :] = jnp.zeros((blk, width), f32)
        dvs[at, :] = jnp.zeros((blk, width), f32)
        return 0

    lax.fori_loop(0, total // blk, prepare, 0)

    def one(z, _):
        first = (z * inner + j) * rows
        low = lax.broadcasted_iota(jnp.int32, (rows, 128), 1) < HEAD
        for t in range(width // 128):
            lanes = slice(128 * t, 128 * t + 128)
            small = (q[z, :, lanes] * 0.125).astype(bf16)
            grad = do[z, :, lanes]
            turned = small.T
            grad_t = grad.T
            prod = grad_t.astype(f32) * ot[z, lanes, :]
            for half in range(2):
                u = 2 * t + half
                qt[u] = half_rows(turned, half)
                dot_t[u] = half_rows(grad_t, half)
                keep = low if half == 0 else ~low
                qz[u] = jnp.where(keep, small, jnp.zeros_like(small))
                dz[u] = jnp.where(keep, grad, jnp.zeros_like(grad))
                rd[u : u + 1, :] = jnp.sum(prod[HEAD * half : HEAD * half + HEAD], 0, keepdims=True)
        dqt[...] = jnp.zeros(dqt.shape, f32)
        for g in range(groups):
            length = lens[g]

            def step(c, masked):
                at = pl.ds(pl.multiple_of(c * span, span), span)
                if masked:
                    key = c * span + lax.broadcasted_iota(jnp.int32, (span, rows), 0)
                    query = first + lax.broadcasted_iota(jnp.int32, (span, rows), 1)
                    allowed = (key <= query) & (key < length)
                for h in range(per):
                    u = UNITS[g][h]
                    lanes = slice(128 * (u // 2), 128 * (u // 2) + 128)
                    span_u = slice(HEAD * u, HEAD * u + HEAD)
                    s = mm(k[at, lanes], qt[u])
                    p = jnp.exp(s - lse[z, u : u + 1, :])
                    if masked:
                        p = jnp.where(allowed, p, 0.0)
                    dp = mm(v[at, lanes], dot_t[u])
                    ds = (p * (dp - rd[u : u + 1, :])).astype(bf16)
                    dvs[at, lanes] += mm(p.astype(bf16), dz[u])
                    dks[at, lanes] += mm(ds, qz[u])
                    dqt[span_u, :] += mm(kt[span_u, at], ds)

            live = first < length
            whole = jnp.where(live, jnp.minimum(first, length) // span, 0)
            count = jnp.where(live, (jnp.minimum(first + rows, length) + span - 1) // span, 0)

            def full_step(c, _):
                step(c, False)
                return 0

            def edge_step(c, _):
                step(c, True)
                return 0

            lax.fori_loop(0, whole, full_step, 0)
            lax.fori_loop(whole, count, edge_step, 0)
        cosine = cos[z]
        sine = sin[z]
        for t in range(width // 128):
            parts = []
            for half in range(2):
                u = 2 * t + half
                a = dqt[HEAD * u : HEAD * u + 32, :] * 0.125
                b = dqt[HEAD * u + 32 : HEAD * u + 64, :] * 0.125
                parts.append(a * cosine + b * sine)
                parts.append(b * cosine - a * sine)
            dq[z, :, 128 * t : 128 * t + 128] = jnp.concatenate(parts, 0).T.astype(bf16)
        return 0

    lax.fori_loop(0, outer, one, 0)

    def finish(i, _):
        at = pl.ds(pl.multiple_of(i * blk, blk), blk)
        dk[at, :] = dks[at, :].astype(bf16)
        dv[at, :] = dvs[at, :].astype(bf16)
        return 0

    lax.fori_loop(0, total // blk, finish, 0)


def attend_back(lens, q, k, v, do, ot, lse, cos, sin, groups, per, inner, span):
    outer, rows, width = q.shape
    units = groups * per
    total = k.shape[0]
    vm = IN_VMEM
    return pl.pallas_call(
        functools.partial(attend_back_kernel, groups, per, span, inner),
        out_shape=(
            jax.ShapeDtypeStruct((outer, rows, width), bf16),
            jax.ShapeDtypeStruct((total, width), bf16),
            jax.ShapeDtypeStruct((total, width), bf16),
        ),
        in_specs=[IN_SMEM] + [vm] * 8,
        out_specs=(vm, vm, vm),
        scratch_shapes=[
            pltpu.VMEM((width, total), bf16),
            pltpu.VMEM((units, 128, rows), bf16),
            pltpu.VMEM((units, 128, rows), bf16),
            pltpu.VMEM((units, rows, 128), bf16),
            pltpu.VMEM((units, rows, 128), bf16),
            pltpu.VMEM((8, rows), f32),
            pltpu.VMEM((width, rows), f32),
            pltpu.VMEM((total, width), f32),
            pltpu.VMEM((total, width), f32),
        ],
        compiler_params=params(),
        name="attend_back",
    )(lens, q, k, v, do, ot, lse, cos, sin)


def middle_kernel(outer, home, tokens, cot, mixture, dots, near, up, down, vecs, lens, mixing, total, mixed, sent, middle_grad, out_term, up_terms, down_terms, sums, attended, middle, hat_s, low_s, low_t, result_s, acc, back, weights, sems):
    tall = tokens.shape[0]
    groups = lens.shape[0]
    rows = tall // groups
    fetch_out = carry(near.at[3], weights.at[0], sems.at[0])
    fetch_up = carry(up, weights.at[pl.ds(1, BLOCKS)], sems.at[1])
    fetch_down = carry(down, weights.at[pl.ds(1 + BLOCKS, BLOCKS)], sems.at[2])
    for g in range(groups):
        tiles = take_heads(lambda o, t: home[o, :, 128 * t : 128 * t + 128].astype(f32), g, outer)
        for i, tile in enumerate(tiles):
            attended[g * rows : g * rows + rows, 128 * i : 128 * i + 128] = tile.astype(bf16)
    fetch_out.wait()
    value = tokens[...].astype(f32) + (mm(attended[...], weights[0]) + vecs[7:8])
    middle[...] = value
    hat, inverse = normalize(value)
    hat_s[...] = hat
    low = (hat * vecs[1:2] + vecs[3:4]).astype(bf16)
    low_s[...] = low
    low_t[...] = low.T
    slots = lax.axis_size("batch") * lax.axis_size("seq") * tall
    scale = slots / total[0].astype(f32)
    row = lax.broadcasted_iota(jnp.int32, (rows, 1), 0) + lax.axis_index("seq") * rows
    live = jnp.concatenate([jnp.where(row < lens[g], scale, 0.0) for g in range(groups)], 0)
    grad = cot[...].astype(f32) * live
    result = (mixing[0] * grad).astype(bf16)
    result_s[...] = result
    sums[...] = jnp.zeros(sums.shape, f32)
    sums[8 + BLOCKS : 9 + BLOCKS] = jnp.sum(result.astype(f32), 0, keepdims=True)
    acc[...] = jnp.zeros(acc.shape, f32)
    back[...] = jnp.zeros(back.shape, f32)
    fetch_up.wait()
    fetch_down.wait()

    def block(i, _):
        up_i = weights[1 + i]
        down_i = weights[1 + BLOCKS + i]
        hidden = mm(low_s[...], up_i) + vecs[pl.ds(8 + i, 1)]
        square = hidden * hidden
        bend = jnp.tanh(0.7978845608028654 * (hidden + 0.044715 * square * hidden))
        half = 0.5 * (1.0 + bend)
        active = (hidden * half).astype(bf16)
        slope = half + 0.5 * hidden * (1.0 - bend * bend) * (0.7978845608028654 * (1.0 + 3.0 * 0.044715 * square))
        acc[...] += mm(active, down_i)
        down_terms[i] = mm(active.T, result_s[...]).astype(bf16)
        hidden_grad = (slope * mm_nt(result_s[...], down_i)).astype(bf16)
        sums[pl.ds(8 + i, 1)] = jnp.sum(hidden_grad.astype(f32), 0, keepdims=True)
        up_terms[i] = mm(low_t[...], hidden_grad).astype(bf16)
        back[...] += mm_nt(hidden_grad, up_i)
        return 0

    lax.fori_loop(0, BLOCKS, block, 0)
    layer_out = middle[...] + acc[...] + vecs[8 + BLOCKS : 9 + BLOCKS]
    mixed[...] = (mixture[...] + mixing[0] * layer_out).astype(bf16)
    grad = cot[...].astype(f32) * live
    sums[VECTORS : VECTORS + 1] = jnp.sum(grad * layer_out, 0, keepdims=True)
    hat = hat_s[...]
    inner_grad = back[...]
    sums[1:2] = jnp.sum(inner_grad * hat, 0, keepdims=True)
    sums[3:4] = jnp.sum(inner_grad, 0, keepdims=True)
    total_grad = mixing[0] * grad + normalize_back(inner_grad, hat, inverse, vecs[1:2])
    middle_grad[...] = total_grad
    branch = total_grad.astype(bf16)
    sums[7:8] = jnp.sum(branch.astype(f32), 0, keepdims=True)
    out_term[...] = mm(attended[...].T, branch).astype(bf16)
    acc[...] = mm_nt(branch, weights[0])

    def write(target, tile, value):
        sent[target, :, 128 * tile : 128 * tile + 128] = value.astype(bf16)

    put_heads(write, lambda g, t: acc[g * rows : g * rows + rows, 128 * t : 128 * t + 128], outer)


def middle_layer(home, tokens, cot, mixture, dots, near, up, down, vecs, lens, mixing, total, outer):
    tall = tokens.shape[0]
    wide = pltpu.VMEM((tall, D), f32)
    low = pltpu.VMEM((tall, D), bf16)
    return pl.pallas_call(
        functools.partial(middle_kernel, outer),
        out_shape=(
            jax.ShapeDtypeStruct((tall, D), bf16),
            jax.ShapeDtypeStruct(home.shape, bf16),
            jax.ShapeDtypeStruct((tall, D), f32),
            jax.ShapeDtypeStruct((D, D), bf16),
            jax.ShapeDtypeStruct((BLOCKS, D, D), bf16),
            jax.ShapeDtypeStruct((BLOCKS, D, D), bf16),
            jax.ShapeDtypeStruct((16, D), f32),
        ),
        in_specs=[IN_VMEM] * 5 + [ANYWHERE] * 3 + [IN_VMEM] + [IN_SMEM] * 3,
        out_specs=(IN_VMEM,) * 7,
        scratch_shapes=[
            low, wide, wide, low, pltpu.VMEM((D, tall), bf16), low, wide, wide,
            pltpu.VMEM((1 + 2 * BLOCKS, D, D), bf16), DMA((3,)),
        ],
        compiler_params=params(),
        name="middle_layer",
    )(home, tokens, cot, mixture, dots, near, up, down, vecs, lens, mixing, total)


def back_kernel(outer, dq, dk, dv, cosine, sine, normed, tokens, near, vecs, cot, lens, mixing, total, middle_grad, out_term, sums, dots, input_grad, terms, small, joined, low_t):
    tall = tokens.shape[0]
    groups = lens.shape[0]
    rows = tall // groups
    for g in range(groups):
        for n, source in enumerate((dq, dk, dv)):
            tiles = take_heads(lambda o, t: source[o, :, 128 * t : 128 * t + 128].astype(f32), g, outer)
            for i, tile in enumerate(tiles):
                if n == 1:
                    tile = turn(tile, cosine[...], -sine[...])
                joined[n, g * rows : g * rows + rows, 128 * i : 128 * i + 128] = tile.astype(bf16)
    low_t[...] = normed[...].T
    small[...] = sums[...]
    back = jnp.zeros((tall, D), f32)
    for n in range(3):
        low = joined[n]
        small[4 + n : 5 + n] = jnp.sum(low.astype(f32), 0, keepdims=True)
        terms[n] = mm(low_t[...], low).astype(bf16)
        back = back + mm_nt(low, near[n])
    terms[3] = out_term[...]
    hat, inverse = normalize(tokens[...].astype(f32))
    small[0:1] = jnp.sum(back * hat, 0, keepdims=True)
    small[2:3] = jnp.sum(back, 0, keepdims=True)
    slots = lax.axis_size("batch") * lax.axis_size("seq") * tall
    scale = slots / total[0].astype(f32)
    row = lax.broadcasted_iota(jnp.int32, (rows, 1), 0) + lax.axis_index("seq") * rows
    live = jnp.concatenate([jnp.where(row < lens[g], scale, 0.0) for g in range(groups)], 0)
    grad = cot[...].astype(f32) * live
    input_grad[...] = mixing[1] * grad + middle_grad[...] + normalize_back(back, hat, inverse, vecs[0:1])
    lane = lax.broadcasted_iota(jnp.int32, (1, D), 1)
    line = jnp.where(lane == 0, jnp.sum(sums[VECTORS : VECTORS + 1], 1, keepdims=True), 0.0)
    for i in range(1, mixing.shape[0]):
        line = line + jnp.where(lane == i, scale * jnp.sum(dots[i : i + 1], 1, keepdims=True), 0.0)
    small[VECTORS : VECTORS + 1] = line


def back_layer(dq, dk, dv, cosine, sine, normed, tokens, near, vecs, cot, lens, mixing, total, middle_grad, out_term, sums, dots, outer):
    tall = tokens.shape[0]
    return pl.pallas_call(
        functools.partial(back_kernel, outer),
        out_shape=(
            jax.ShapeDtypeStruct((tall, D), f32),
            jax.ShapeDtypeStruct((4, D, D), bf16),
            jax.ShapeDtypeStruct((16, D), f32),
        ),
        in_specs=[IN_VMEM] * 10 + [IN_SMEM] * 3 + [IN_VMEM] * 4,
        out_specs=(IN_VMEM,) * 3,
        scratch_shapes=[pltpu.VMEM((3, tall, D), bf16), pltpu.VMEM((D, tall), bf16)],
        compiler_params=params(),
        name="back_layer",
    )(dq, dk, dv, cosine, sine, normed, tokens, near, vecs, cot, lens, mixing, total, middle_grad, out_term, sums, dots)


def adam(param, grad, first, second, decay):
    first_new = beta_one * first + (1.0 - beta_one) * grad
    second_new = beta_two * second + (1.0 - beta_two) * grad * grad
    fix_one = 1.0 - beta_one**adam_step
    fix_two = 1.0 - beta_two**adam_step
    update = first_new / fix_one / (jnp.sqrt(second_new / fix_two) + adam_eps)
    return (-learn_rate * (update + decay * param), first_new)


def adam_kernel(near, up, down, *refs):
    given, results = refs[:12], refs[12:]
    starts = (0, 3, 0, None)
    for n in range(4):
        param, first, second = given[3 * n : 3 * n + 3]
        grad_out, step_out, first_out = results[3 * n : 3 * n + 3]
        count = param.shape[1] // D if n < 3 else 1
        for i in range(count):
            lanes = slice(i * D, i * D + D)
            grad = down[...] if n == 3 else (up if n == 2 else near)[starts[n] + i]
            grad_out[:, lanes] = grad
            step_out[:, lanes], first_out[:, lanes] = adam(param[:, lanes], grad, first[:, lanes], second[:, lanes], decay_rate)


def adam_all(near, up, down, given):
    shapes = []
    for n in range(4):
        shapes += [jax.ShapeDtypeStruct(given[3 * n].shape, f32)] * 3
    return pl.pallas_call(
        adam_kernel,
        out_shape=tuple(shapes),
        in_specs=[IN_VMEM] * 15,
        out_specs=(IN_VMEM,) * 12,
        compiler_params=params(),
        name="adam_all",
    )(near, up, down, *given)


def summed(into, index, more, other):
    into[index] = (into[index].astype(f32) + more[other].astype(f32)).astype(bf16)


def fold_kernel(batches, inner, with_rest, *refs):
    refs = list(refs)

    def take(n):
        got = refs[:n]
        del refs[:n]
        return got

    dq, dk, dv = take(3)
    terms = take(2) if with_rest else []
    dq_all, dk_all, dv_all = take(3)
    rest_out = take(2) if with_rest else []
    cbuf, xbuf, done, qs, qr, zs, zr, xs, xr, cs, cr, local = take(12)
    outer = dq.shape[0]
    across = inner // 2
    here = Place(batches, outer, inner)
    o, a, b, c = here.o, here.a, here.batch, here.c
    greet(here.z_peers[1:] + here.x_peers[1:] + [here.twin] + (here.y_peers[1:] if with_rest else []))
    waits = [carry(dq.at[o], dq_all.at[o], local.at[0])]
    given = (dk, dv)
    results = (dk_all, dv_all)
    order = [t % outer for t in range(1, outer + 1)]
    xorder = list(range(1, across)) + [0]
    yorder = list(range(1, batches)) + [0]
    to_twin, rest_over = {}, {}

    def give_block(t):
        for i in (0, 1):
            for d in xorder:
                z, x = here.zs[t], here.xs[d]
                to_twin[i, t, d] = push(given[i].at[z, x * 2 + 1 - c], cbuf.at[i, z, x], cs.at[i, t, d], cr.at[i, t, d], here.twin)

    if with_rest:
        bufs = (refs[0:3], refs[3:6])
        rest_sem, rcs, rcr, rys, ryr, rxs, rxr = refs[6:]

    def theirs(i, y, x, core):
        if i == 0:
            return terms[0].at[pl.ds(2 * core, 2), y, :, x]
        return terms[1].at[y, :, x, core]

    def give_rest(i, dy, dx):
        y, x = here.ys[dy], here.xs[dx]
        rest_over["c", i, dy, dx] = push(theirs(i, y, x, 1 - c), bufs[i][0].at[y, x], rcs.at[i, dy, dx], rcr.at[i, dy, dx], here.twin)

    give_block(order[0])
    if with_rest:
        for dy in yorder:
            for dx in xorder:
                for i in (0, 1):
                    give_rest(i, dy, dx)
    for t in order[1:]:
        give_block(t)
    for t in range(1, outer):
        waits.append(push(dq.at[here.zs[t]], dq_all.at[o], qs.at[t], qr.at[t], here.z_peers[t]))
    over = {}

    def fold_block(t):
        for i in (0, 1):
            for d in xorder:
                to_twin[i, t, d].wait()
                z, x = here.zs[t], here.xs[d]
                summed(cbuf, (i, z, x), given[i], (z, x * 2 + c))
                if d:
                    over[i, t, d] = push(cbuf.at[i, z, x], xbuf.at[i, z, d], xs.at[i, t, d], xr.at[i, t, d], here.x_peers[d])

    def finish_block(t):
        for i in (0, 1):
            z = here.zs[t]
            total = cbuf[i, z, a].astype(f32)
            for d in range(1, across):
                over[i, t, d].wait()
                total = total + xbuf[i, z, d].astype(f32)
            done[i, z] = total.astype(bf16)
            if t:
                waits.append(push(done.at[i, z], results[i].at[o], zs.at[i, t], zr.at[i, t], here.z_peers[t]))
            else:
                waits.append(carry(done.at[i, z], results[i].at[o], local.at[1 + i]))

    def each(i, add):
        if i == 0:

            def one(n, _):
                add((lax.div(n, outer), lax.rem(n, outer)))
                return 0

            lax.fori_loop(0, 2 * outer, one, 0)
        else:

            def one(z, _):
                add((z,))
                return 0

            lax.fori_loop(0, outer, one, 0)

    def rest_core(dy, dx):
        y, x = here.ys[dy], here.xs[dx]
        for i in (0, 1):
            rest_over["c", i, dy, dx].wait()
            into = bufs[i][0]
            if i == 0:
                each(0, lambda at: summed(into, (y, x) + at, terms[0], (2 * c + at[0], y, at[1], x)))
            else:
                each(1, lambda at: summed(into, (y, x) + at, terms[1], (y, at[0], x, c)))
            if dy:
                rest_over["y", i, dy, dx] = push(into.at[y, x], bufs[i][1].at[dy, dx], rys.at[i, dy, dx], ryr.at[i, dy, dx], here.y_peers[dy])

    def rest_y(dx):
        x = here.xs[dx]
        for i in (0, 1):
            into, more = bufs[i][0], bufs[i][1]
            for dy in range(1, batches):
                rest_over["y", i, dy, dx].wait()
                each(i, lambda at: summed(into, (b, x) + at, more, (dy, dx) + at))
            if dx:
                rest_over["x", i, dx] = push(into.at[b, x], bufs[i][2].at[dx], rxs.at[i, dx], rxr.at[i, dx], here.x_peers[dx])

    fold_block(order[0])
    if with_rest:
        for dy in yorder[:-1]:
            for dx in xorder:
                rest_core(dy, dx)
    fold_block(order[1])
    finish_block(order[0])
    if with_rest:
        for dx in xorder:
            rest_core(0, dx)
    for n in range(2, outer):
        fold_block(order[n])
        finish_block(order[n - 1])
        if with_rest and n == 2:
            for dx in xorder[:-1]:
                rest_y(dx)
    finish_block(order[-1])
    if with_rest:
        rest_y(0)
        for i in (0, 1):
            into, more = bufs[i][0], bufs[i][2]
            for d in range(1, across):
                rest_over["x", i, d].wait()
                each(i, lambda at: summed(into, (b, a) + at, more, (d,) + at))
            waits.append(carry(into.at[b, a], rest_out[i], rest_sem.at[i]))
    for copy in waits:
        copy.wait()


def fold_heads(dq, dk, dv, terms, batches, inner, ident):
    outer, rows, width = dq.shape
    across = inner // 2
    piece = jax.ShapeDtypeStruct(dq.shape, dq.dtype)
    with_rest = bool(terms)
    shapes = (piece, piece, piece)
    scratch = [pltpu.VMEM((2, outer, across, rows, width), bf16)] * 2 + [pltpu.VMEM((2, outer, rows, width), bf16)]
    scratch += [DMA((outer,))] * 2 + [DMA((2, outer))] * 2 + [DMA((2, outer, across))] * 4 + [DMA((3,))]
    if with_rest:
        for tail in ((2, outer) + terms[0].shape[4:], (outer,) + terms[1].shape[4:]):
            shapes += (jax.ShapeDtypeStruct(tail, bf16),)
            scratch += [pltpu.VMEM((batches, across) + tail, bf16)] * 2 + [pltpu.VMEM((across,) + tail, bf16)]
        scratch += [DMA((2,))]
        scratch += [DMA((2, batches, across))] * 4 + [DMA((2, across))] * 2
    return pl.pallas_call(
        functools.partial(fold_kernel, batches, inner, with_rest),
        out_shape=shapes,
        in_specs=[ANYWHERE] + [IN_VMEM] * (2 + len(terms)),
        out_specs=(ANYWHERE,) * len(shapes),
        scratch_shapes=scratch,
        compiler_params=remote_params(ident, ROOM),
        name="fold_heads",
    )(dq, dk, dv, *terms)


def last_kernel(batches, outer, inner, *refs):
    refs = list(refs)

    def take(n):
        got = refs[:n]
        del refs[:n]
        return got

    terms, up_line, down_line, small = take(4)
    near_out, up_out, down_out, small_out = take(4)
    rc, ry, rx, rz, uz, dz, kept, sc, sx, sy, sz = take(11)
    cs, cr, ys, yr, xs, xr, zs, zr, us, ur, ds, dr, fs, fr, ss, sr = refs
    across = inner // 2
    here = Place(batches, outer, inner)
    o, a, b, c = here.o, here.a, here.batch, here.c
    share = near_out.shape[1]
    greet(here.z_peers[1:] + here.x_peers[1:] + here.y_peers[1:] + [here.twin])
    xorder = list(range(1, across)) + [0]
    yorder = list(range(1, batches)) + [0]
    over = {}
    for p, dy, dx in [(p, dy, dx) for dy in yorder for dx in xorder for p in (0, 1)]:
        y, x = here.ys[dy], here.xs[dx]
        over["c", p, dy, dx] = push(terms.at[2 * (1 - c) + p, y, :, x], rc.at[p, y, x], cs.at[p, dy, dx], cr.at[p, dy, dx], here.twin)
    small_copy = push(small, sc, ss.at[0], sr.at[0], here.twin)
    line_copies = {}
    for t in range(1, outer):
        line_copies[0, t] = push(up_line.at[:, here.zs[t]], uz.at[t], us.at[t], ur.at[t], here.z_peers[t])
        line_copies[1, t] = push(down_line.at[here.zs[t]], dz.at[t], ds.at[t], dr.at[t], here.z_peers[t])

    def add_all(into_at, more, more_at):
        def one(z, _):
            summed(rc, into_at + (z,), more, more_at(z))
            return 0

        lax.fori_loop(0, outer, one, 0)

    def core(p, dy, dx):
        y, x = here.ys[dy], here.xs[dx]
        over["c", p, dy, dx].wait()
        add_all((p, y, x), terms, lambda z: (2 * c + p, y, z, x))
        if p == 0 and dy:
            over["y", 0, dy, dx] = push(rc.at[0, y, x], ry.at[0, dy, dx], ys.at[0, dy, dx], yr.at[0, dy, dx], here.y_peers[dy])
        if p == 1 and dx:
            over["x", 1, dy, dx] = push(rc.at[1, y, x], rx.at[1, dx, dy], xs.at[1, dy, dx], xr.at[1, dy, dx], here.x_peers[dx])

    for dy in yorder:
        for dx in xorder:
            for p in (0, 1):
                core(p, dy, dx)
    small_copy.wait()
    sc[...] = sc[...] + small[...]
    small_x = [push(sc, sx.at[a], ss.at[d], sr.at[d], here.x_peers[d]) for d in range(1, across)]
    sx[a] = sc[...]
    for dx in xorder:
        x = here.xs[dx]
        for dy in range(1, batches):
            over["y", 0, dy, dx].wait()
            add_all((0, b, x), ry, lambda z: (0, dy, dx, z))
        if dx:
            over["x", 0, 0, dx] = push(rc.at[0, b, x], rx.at[0, dx, 0], xs.at[0, 0, dx], xr.at[0, 0, dx], here.x_peers[dx])
    for dy in yorder:
        y = here.ys[dy]
        for dx in range(1, across):
            over["x", 1, dy, dx].wait()
            add_all((1, y, a), rx, lambda z: (1, dx, dy, z))
        if dy:
            over["y", 1, dy, 0] = push(rc.at[1, y, a], ry.at[1, dy, 0], ys.at[1, dy, 0], yr.at[1, dy, 0], here.y_peers[dy])
    for copy in small_x:
        copy.wait()
    total = sx[0]
    for x in range(1, across):
        total = total + sx[x]
    sc[...] = total
    sy[b] = total
    small_y = [push(sc, sy.at[b], ss.at[across + d], sr.at[across + d], here.y_peers[d]) for d in range(1, batches)]
    z_copies = {}
    for dx in range(1, across):
        over["x", 0, 0, dx].wait()
        add_all((0, b, a), rx, lambda z: (0, dx, 0, z))
    for t in range(1, outer):
        z_copies[0, t] = push(rc.at[0, b, a, here.zs[t]], rz.at[0, t], zs.at[0, t], zr.at[0, t], here.z_peers[t])
    for dy in range(1, batches):
        over["y", 1, dy, 0].wait()
        add_all((1, b, a), ry, lambda z: (1, dy, 0, z))
    for t in range(1, outer):
        z_copies[1, t] = push(rc.at[1, b, a, here.zs[t]], rz.at[1, t], zs.at[1, t], zr.at[1, t], here.z_peers[t])
    for copy in small_y:
        copy.wait()
    total = sy[0]
    for y in range(1, batches):
        total = total + sy[y]
    sc[...] = total
    sz[o] = total
    small_z = [
        push(sc, sz.at[o], ss.at[across + batches + t], sr.at[across + batches + t], here.z_peers[t]) for t in range(1, outer)
    ]
    sums = down_line[o].astype(f32)
    for t in range(1, outer):
        line_copies[1, t].wait()
        sums = sums + dz[t].astype(f32)
    down_out[...] = sums
    for t in range(1, outer):
        line_copies[0, t].wait()
    give = pl.multiple_of(share * (1 - c), 8)
    rest_sends, near_sends = [], []
    for p in (0, 1):
        sums = up_line[p, o].astype(f32)
        for t in range(1, outer):
            sums = sums + uz[t, p].astype(f32)
        kept[1, p] = sums
    rest_sends.append(push(kept.at[1, :, pl.ds(give, share)], up_out.at[pl.ds(2 * c, 2)], fs.at[1], fr.at[1], here.twin))
    for p in (0, 1):
        sums = rc[p, b, a, o].astype(f32)
        for t in range(1, outer):
            z_copies[p, t].wait()
            sums = sums + rz[p, t].astype(f32)
        kept[0, p] = sums
    near_sends.append(push(kept.at[0, :, pl.ds(give, share)], near_out.at[pl.ds(2 * c, 2)], fs.at[0], fr.at[0], here.twin))
    for p in (0, 1):
        for kind, dest in enumerate((near_out, up_out)):
            value = kept[kind, p]
            dest[2 * c + p] = jnp.where(c == 0, value[:share], value[share:])
    for copy in small_z:
        copy.wait()
    total = sz[0]
    for z in range(1, outer):
        total = total + sz[z]
    small_out[...] = total
    for copy in rest_sends + near_sends:
        copy.wait()


def reduce_last(terms, up_line, down_line, small, batches, outer, inner, ident):
    across = inner // 2
    tail = terms.shape[4:]
    share = tail[0] // 2
    buf = pltpu.VMEM
    scratch = [
        buf((2, batches, across, outer) + tail, bf16),
        buf((2, batches, across, outer) + tail, bf16),
        buf((2, across, batches, outer) + tail, bf16),
        buf((2, outer) + tail, bf16),
        buf((outer, 2) + tail, bf16),
        buf(down_line.shape, bf16),
        buf((2, 2) + tail, f32),
        buf(small.shape, f32),
        buf((across,) + small.shape, f32),
        buf((batches,) + small.shape, f32),
        buf((outer,) + small.shape, f32),
    ]
    scratch += [DMA((2, batches, across))] * 6 + [DMA((2, outer))] * 2 + [DMA((outer,))] * 4 + [DMA((2,))] * 2
    scratch += [DMA((across + batches + outer,))] * 2
    return pl.pallas_call(
        functools.partial(last_kernel, batches, outer, inner),
        out_shape=(
            jax.ShapeDtypeStruct((4, share, D), f32),
            jax.ShapeDtypeStruct((4, share, D), f32),
            jax.ShapeDtypeStruct(down_line.shape[1:], f32),
            jax.ShapeDtypeStruct(small.shape, f32),
        ),
        in_specs=[IN_VMEM] * 4,
        out_specs=(IN_VMEM,) * 4,
        scratch_shapes=scratch,
        compiler_params=remote_params(ident, ROOM),
        name="reduce_last",
    )(terms, up_line, down_line, small)


def body(
    tokens_in,
    earlier_outs,
    out_cotangent,
    seq_lengths,
    qkv_weight,
    out_weight,
    up_weight,
    down_weight,
    qkv_first,
    qkv_second,
    out_first,
    out_second,
    up_first,
    up_second,
    down_first,
    down_second,
    small_params,
    small_first,
    small_second,
):
    groups, rows, _ = tokens_in.shape
    tall = groups * rows
    batches = lax.axis_size("batch")
    seq_count = lax.axis_size("seq")
    seq_rank = lax.axis_index("seq")
    devices = batches * seq_count
    outer = math.gcd(seq_count, D // HEAD)
    inner = seq_count // outer
    per = D // HEAD // outer
    length = seq_count * rows
    width = groups * per * HEAD
    share = D // devices
    remote = share % 8 == 0
    everywhere = ("batch", "seq")
    grid = (batches, outer, inner // 2)

    tokens = tokens_in.reshape(tall, D)
    cot = out_cotangent.reshape(tall, D)
    earlier = earlier_outs.reshape(-1, tall, D)
    vecs = jnp.pad(small_params[: VECTORS * D].reshape(VECTORS, D), ((0, 16 - VECTORS), (0, 0)))
    mixing = small_params[VECTORS * D :]
    mine = jnp.sum(seq_lengths)

    freq = 10000.0 ** (-jnp.arange(HEAD // 2, dtype=f32) * 2.0 / HEAD)
    query_pos = seq_rank * rows + jnp.arange(rows, dtype=jnp.int32)
    turned = query_pos.astype(f32)[:, None] * freq[None, :]
    cosine, sine = jnp.cos(turned), jnp.sin(turned)
    cosine = jnp.concatenate([cosine] * 4, 1)
    sine = jnp.concatenate([-sine, sine] * 2, 1)
    block_pos = (jnp.arange(outer) * inner + seq_rank % inner)[:, None] * rows + jnp.arange(rows)[None, :]
    block_turned = block_pos.astype(f32)[:, None, :] * freq[None, :, None]
    block_cos, block_sin = jnp.cos(block_turned), jnp.sin(block_turned)

    def by_rows(shard):
        return shard.astype(bf16).reshape(share, -1, D).transpose(1, 0, 2)

    def by_blocks(gathered):
        return gathered.transpose(1, 0, 2, 3).reshape(-1, D, D)

    if remote:
        near, up_line, down_line, counts, normed, mixture, dots = gather_first(
            qkv_weight, out_weight, up_weight, down_weight, seq_lengths, mixing, tokens, cot, earlier, vecs,
            jnp.full((8, 128), mine, jnp.int32), batches, outer, inner, 1,
        )
        near = near.reshape(4, D, D)
        total = jnp.sum(counts[:, 0, 0]).reshape(1)
        q, k, v, up, down = spread_heads(normed, near, vecs, cosine, sine, (up_line, down_line), batches, outer, inner, 2)
        up, down = up.reshape(BLOCKS, D, D), down.reshape(BLOCKS, D, D)
    else:
        near = by_blocks(lax.all_gather(jnp.concatenate([by_rows(qkv_weight), by_rows(out_weight)], 0), everywhere, axis=0))
        up = by_blocks(lax.all_gather(by_rows(up_weight), everywhere, axis=0))
        down = lax.all_gather(down_weight.astype(bf16), everywhere, axis=0).reshape(BLOCKS, D, D)
        total = lax.psum(mine, "batch").reshape(1)
        wide = tokens.astype(f32)
        normed = (normalize(wide)[0] * vecs[0] + vecs[2]).astype(bf16)
        live = (query_pos[None, :] < seq_lengths[:, None]).astype(f32).reshape(tall, 1)
        terms = [tokens] + [earlier[i] for i in range(earlier.shape[0])]
        mixture = sum(mixing[1 + i] * term.astype(f32) for i, term in enumerate(terms))
        sums = [jnp.sum(cot.astype(f32) * live * term.astype(f32), 0) for term in terms]
        dots = jnp.pad(jnp.stack(sums), ((1, 15 - len(sums)), (0, 0)))
        q, k, v = spread_heads(normed, near, vecs, cosine, sine, (), batches, outer, inner, 2)

    k, v = k.reshape(length, width), v.reshape(length, width)
    attended, turned_out, log_total = attend(seq_lengths, q, k, v, groups, per, inner, math.gcd(length, 1024))
    home = swap_outer(attended, batches, inner, 3)
    mixed, sent, middle_grad, out_term, up_terms, down_terms, sums = middle_layer(
        home, tokens, cot, mixture, dots, near, up, down, vecs, seq_lengths, mixing, total, outer
    )
    grad_mine = swap_outer(sent, batches, inner, 4)
    dq, dk, dv = attend_back(
        seq_lengths, q, k, v, grad_mine, turned_out, log_total, block_cos, block_sin, groups, per, inner, math.gcd(length, 512)
    )
    pieces = (outer, inner, rows, width)
    dk, dv = dk.reshape(pieces), dv.reshape(pieces)
    if remote:
        blocked = (up_terms.reshape((4,) + grid + (2 * share, D)), down_terms.reshape(grid + (2, BLOCKS * share, D)))
        dq, dk, dv, up_back, down_back = fold_heads(dq, dk, dv, blocked, batches, inner, 5)
    else:
        dq, dk, dv = fold_heads(dq, dk, dv, (), batches, inner, 5)
    input_grad, near_terms, small = back_layer(
        dq, dk, dv, cosine, sine, normed, tokens, near, vecs, cot, seq_lengths, mixing, total, middle_grad, out_term, sums, dots, outer
    )
    if remote:
        near_grad, up_grad, down_grad, small = reduce_last(
            near_terms.reshape((4,) + grid + (2 * share, D)), up_back, down_back, small, batches, outer, inner, 6
        )
    else:

        def scattered(terms):
            return lax.psum_scatter(terms.reshape(-1, devices, share, D), everywhere, scatter_dimension=1).astype(f32)

        near_grad, up_grad = scattered(near_terms), scattered(up_terms)
        down_grad = lax.psum_scatter(down_terms.reshape(devices, -1, D), everywhere, scatter_dimension=0).astype(f32)
        small = lax.psum(small, everywhere)
    small_grad = small.reshape(-1)[: small_params.shape[0]]
    small_step, small_first_new = adam(small_params, small_grad, small_first, small_second, 0.0)
    (
        qkv_grad, qkv_step, qkv_first_new, out_grad, out_step, out_first_new,
        up_grad, up_step, up_first_new, down_grad, down_step, down_first_new,
    ) = adam_all(
        near_grad, up_grad, down_grad,
        (qkv_weight, qkv_first, qkv_second, out_weight, out_first, out_second,
         up_weight, up_first, up_second, down_weight, down_first, down_second),
    )
    return (
        mixed.reshape(tokens_in.shape),
        input_grad.reshape(tokens_in.shape),
        qkv_grad,
        out_grad,
        up_grad,
        down_grad,
        small_grad,
        qkv_step,
        out_step,
        up_step,
        down_step,
        small_step,
        qkv_first_new,
        out_first_new,
        up_first_new,
        down_first_new,
        small_first_new,
    )


def solution(mesh):
    placed = (
        P("batch", "seq", None),
        P(None, "batch", "seq", None),
        P("batch", "seq", None),
        P("batch"),
        P(("batch", "seq"), None),
        P(("batch", "seq"), None),
        P(("batch", "seq"), None),
        P(("batch", "seq"), None),
        P(("batch", "seq"), None),
        P(("batch", "seq"), None),
        P(("batch", "seq"), None),
        P(("batch", "seq"), None),
        P(("batch", "seq"), None),
        P(("batch", "seq"), None),
        P(("batch", "seq"), None),
        P(("batch", "seq"), None),
        P(),
        P(),
        P(),
    )
    return jax.shard_map(
        body,
        mesh=mesh,
        in_specs=placed,
        out_specs=(
            P("batch", "seq", None),
            P("batch", "seq", None),
            P(("batch", "seq"), None),
            P(("batch", "seq"), None),
            P(("batch", "seq"), None),
            P(("batch", "seq"), None),
            P(),
            P(("batch", "seq"), None),
            P(("batch", "seq"), None),
            P(("batch", "seq"), None),
            P(("batch", "seq"), None),
            P(),
            P(("batch", "seq"), None),
            P(("batch", "seq"), None),
            P(("batch", "seq"), None),
            P(("batch", "seq"), None),
            P(),
        ),
        check_vma=False,
    )
```

profile of v0, /device:TPU:0, one launch (start us, length us, event | category | flops | bytes accessed | tf_op | source)
XLA Modules:
  0.0 413.6 jit_solution(15586470123565546469)
XLA Ops:
  0.7 0.5 fusion
  1.2 1.0 pad_maximum_fusion
  2.2 0.8 reshape.133
  3.0 0.6 pad.4.refs_9_.refs_2_.vecs
  3.6 1.2 slice.12.refs_5_.mixing
  4.8 1.3 reduce_sum.18
  6.1 1.2 broadcast_in_dim.2.refs_10_
  7.3 52.1 %gather_first.1 = (bf16[4,2,4,2,48,768]{5,4,3,2,1,0:T(8,128)(2,1)}, bf16[2,4,48,768]{3,2,1,0:T(8,128)(2,1)}, bf16[4,96,768]{2,1,0:T(8,128)(2,1)}, s32[2,8,128]{2...) custom-call(f32[24,2304]{1,0:T(8,128)} %refs_0_.3, f32[24,768]{1,0:T(8,128)} %refs_3_.3, ...), custom_call_target="tpu_custom_call" | custom-call | tf_op jit(solution)/shard_map/gather_first/pallas_call | solution.py:291
  59.4 71.5 %spread_heads.1 = (bf16[4,256,384]{2,1,0:T(8,128)(2,1)}, bf16[4,4,256,384]{3,2,1,0:T(8,128)(2,1)}, bf16[4,4,256,384]{3,2,1,0:T(8,128)(2,1)}, bf16[4,2,4,2,48,768...) custom-call(bf16[512,768]{1,0:T(8,128)(2,1)} %get-tuple-element.66.refs_0_.normed, bf16[4,768,768]{2,1,0:T(8,128)(2,1)} %bitcast.17, ...), custom_call_target="tpu_custom_call" | custom-call | tf_op jit(solution)/shard_map/spread_heads/pallas_call | solution.py:439
  130.9 30.0 %attend.1 = (bf16[4,256,384]{2,1,0:T(8,128)(2,1)}, f32[4,384,256]{2,1,0:T(8,128)}, f32[4,8,256]{2,1,0:T(8,128)}) custom-call(s32[2]{0:T(128)} %lens.7, bf16[4,256,384]{2,1,0:T(8,128)(2,1)} %get-tuple-element.70.q, bf16[4096,384]{1,0:T(8,128)(2,1)} %bitcast.20, bf16[4096,384]{1,0:T(8,128)(2,1)} %bitcast.22), custom_call_target="tpu_custom_call" | custom-call | tf_op jit(solution)/shard_map/attend/pallas_call | solution.py:571
  160.9 17.9 %swap_heads.2.home = bf16[4,256,384]{2,1,0:T(8,128)(2,1)} custom-call(bf16[4,256,384]{2,1,0:T(8,128)(2,1)} %get-tuple-element.73.x), custom_call_target="tpu_custom_call" | custom-call | tf_op jit(solution)/shard_map/swap_heads/pallas_call | solution.py:465
  178.8 1.3 slice_reduce_fusion
  180.2 29.7 %middle_layer.1 = (bf16[512,768]{1,0:T(8,128)(2,1)}, bf16[4,256,384]{2,1,0:T(8,128)(2,1)}, f32[512,768]{1,0:T(8,128)}, bf16[768,768]{1,0:T(8,128)(2,1)}, bf16[4,...) custom-call(bf16[4,256,384]{2,1,0:T(8,128)(2,1)} %swap_heads.2.home, ...), custom_call_target="tpu_custom_call" | custom-call | tf_op jit(solution)/shard_map/middle_layer/pallas_call | solution.py:795
  209.9 20.5 %swap_heads.3.do = bf16[4,256,384]{2,1,0:T(8,128)(2,1)} custom-call(bf16[4,256,384]{2,1,0:T(8,128)(2,1)} %get-tuple-element.80.x), custom_call_target="tpu_custom_call" | custom-call | tf_op jit(solution)/shard_map/swap_heads/pallas_call | solution.py:465
  230.4 0.1 add_convert_fusion
  230.5 1.2 multiply_sine_fusion
  231.7 32.2 %attend_back.1 = (bf16[4,256,384]{2,1,0:T(8,128)(2,1)}, bf16[4096,384]{1,0:T(8,128)(2,1)}, bf16[4096,384]{1,0:T(8,128)(2,1)}) custom-call(s32[2]{0:T(128)} %lens.7, bf16[4,256,384]{2,1,0:T(8,128)(2,1)} %get-tuple-element.70.q, bf16[4096,384]{1,0:T(8,128)(2,1)} %bitcast.21, bf16[4096,384]{1,0:T(8,128)(2,1)} %bitcast.23, bf16[4,256,384]{2,1,0:T(8,128)(2,1)} %swap_heads.3.do, ...), custom_call_target="tpu_custom_call" | custom-call | tf_op jit(solution)/shard_map/attend_back/pallas_call | solution.py:694
  264.0 82.5 %fold_heads.1 = (bf16[4,256,384]{2,1,0:T(8,128)(2,1)}, bf16[4,256,384]{2,1,0:T(8,128)(2,1)}, bf16[4,256,384]{2,1,0:T(8,128)(2,1)}, bf16[2,4,48,768]{3,2,1,0:T(8,128)(2,1)}, bf16[4,96,768]{2,1,0:T(8,128)(2,1)}) custom-call(bf16[4,256,384]{2,1,0:T(8,128)(2,1)} %get-tuple-element.83.refs_0_, bf16[4,4,256,384]{3,2,1,0:T(8,128)(2,1)} %bitcast.36, ...), custom_call_target="tpu_custom_call" | custom-call | tf_op jit(solution)/shard_map/fold_heads/pallas_call | solution.py:1071
  346.5 12.8 %back_layer.1 = (f32[512,768]{1,0:T(8,128)}, bf16[4,768,768]{2,1,0:T(8,128)(2,1)}, f32[16,768]{1,0:T(8,128)}) custom-call(bf16[4,256,384]{2,1,0:T(8,128)(2,1)} %get-tuple-element.88.dq, bf16[4,256,384]{2,1,0:T(8,128)(2,1)} %get-tuple-element.89.dk, bf16[4,256,384]{2,1,0:T(8,128)(2,1)} %get-tuple-element.90.dv, f32[256,128]{1,0:T(8,128)} %get-tuple-element.123.refs_3_.cosine, ...), custom_call_target="tpu_custom_call" | custom-call | tf_op jit(solution)/shard_map/back_layer/pallas_call | solution.py:855
  359.3 49.4 %reduce_last.1 = (f32[4,24,768]{2,1,0:T(8,128)}, f32[4,24,768]{2,1,0:T(8,128)}, f32[96,768]{1,0:T(8,128)}, f32[16,768]{1,0:T(8,128)}) custom-call(bf16[4,2,4,2,48,768]{5,4,3,2,1,0:T(8,128)(2,1)} %bitcast.31, bf16[2,4,48,768]{3,2,1,0:T(8,128)(2,1)} %get-tuple-element.96.refs_1_, bf16[4,96,768]{2,1,0:T(8,128)(2,1)} %get-tuple-element.97.refs_2_, ...), custom_call_target="tpu_custom_call" | custom-call | tf_op jit(solution)/shard_map/reduce_last/pallas_call | solution.py:1234
  408.7 0.0 copy-start
  408.7 0.0 copy-start.2
  408.8 3.7 adam_all.1
  412.5 0.7 fusion.7
  (10 shorter events, 0.0 us)
Async XLA Ops:
  408.7 3.8 copy-start.1
  408.7 3.8 copy-start
  408.7 3.8 copy-start.2
  408.7 3.8 copy-start.3
where the time goes:
time: 422 us; the launch traced here: 414 us
  Pallas kernels  402 us (95%)
  other arithmetic  6.14 us (1%)
    pallas_call x1, Pallas kernels, fold_heads(): pl.pallas_call(functools.partial(fold_kernel, batches, inner, with_rest),...  82.5 us
    pallas_call x1, Pallas kernels, spread_heads(): pl.pallas_call(functools.partial(spread_kernel, batches, outer, inner, wi...  71.5 us
    pallas_call x1, Pallas kernels, gather_first(): pl.pallas_call(functools.partial(first_kernel, batches, outer, inner, fir...  52.1 us
    pallas_call x1, Pallas kernels, reduce_last(): pl.pallas_call(functools.partial(last_kernel, batches, outer, inner), out...  49.4 us
    pallas_call x2, Pallas kernels, swap_outer(): pl.pallas_call(functools.partial(swap_kernel, batches, inner), out_shape=...  38.4 us
    pallas_call x1, Pallas kernels, attend_back(): pl.pallas_call(functools.partial(attend_back_kernel, groups, per, span, i...  32.2 us
    pallas_call x1, Pallas kernels, attend(): pl.pallas_call(functools.partial(attend_kernel, groups, per, span, inner)...  30 us
    pallas_call x1, Pallas kernels, middle_layer(): pl.pallas_call(functools.partial(middle_kernel, outer), out_shape=(jax.Sh...  29.7 us

commit v1 on v0

--- a/solution.py
+++ b/solution.py
@@ -143,6 +143,42 @@
     return tiles
 
 
+def fold_single(value, odd):
+    half = value.shape[0] // 2
+    top, bottom = value[:half], value[half:]
+    lane = lax.broadcasted_iota(jnp.int32, top.shape, 1)
+    if odd:
+        return jnp.where(lane < HEAD, pltpu.roll(top, HEAD, 1), bottom)
+    return jnp.where(lane < HEAD, top, pltpu.roll(bottom, HEAD, 1))
+
+
+def unfold_single(value, high):
+    turned = pltpu.roll(value, HEAD, 1)
+    return jnp.concatenate([turned, value] if high else [value, turned], 0)
+
+
+def unfold_heads(read, rows, outer):
+    tiles = [None] * (outer * 3 // 2)
+    for o in range(0, outer, 2):
+        base = 3 * o * HEAD // 128
+        first, second = read(o), read(o + 1)
+        tiles[base] = first[:rows]
+        tiles[base + 2] = second[:rows]
+        low, high = unfold_single(first[rows:], False), unfold_single(second[rows:], True)
+        lane = lax.broadcasted_iota(jnp.int32, low.shape, 1)
+        tiles[base + 1] = jnp.where(lane < HEAD, low, high)
+    return tiles
+
+
+def fold_heads_of(write, tile_of, outer):
+    for o in range(outer):
+        first = 3 * o * HEAD
+        odd = first % 128 != 0
+        pair = (first + HEAD if odd else first) // 128
+        single = (first if odd else first + 128) // 128
+        write(o, jnp.concatenate([tile_of(pair), fold_single(tile_of(single), odd)], 0))
+
+
 def first_kernel(batches, outer, inner, first_row, *refs):
     refs = list(refs)
 
@@ -151,9 +187,9 @@
         del refs[:n]
         return got
 
-    qkv, out, up, down, lens, mixing, tokens, cot, earlier, vecs, count = take(11)
+    qkv, out, up, down, lens, mixing, tokens, cot, earlier, vecs = take(10)
     near_all, up_line, down_line, counts, normed, mixture, dots = take(7)
-    own, got, near, up_bit, down_bit, queue = take(6)
+    own, got, near, up_bit, down_bit, queue, count = take(7)
     zs, zr, xs, xr, ys, yr, cs, cr, us, ur, ds, dr, ns, nr, ts, tr, local, es = refs
     across = inner // 2
     here = Place(batches, outer, inner)
@@ -167,6 +203,10 @@
     for block in range(4):
         own[block] = qkv[:, block * D : block * D + D] if block < 3 else out[...]
         own[4 + block] = up[:, block * D : block * D + D]
+    here_count = lens[0]
+    for g in range(1, groups):
+        here_count = here_count + lens[g]
+    count[...] = jnp.zeros(count.shape, jnp.int32) + here_count
     greet(here.z_peers[1:] + here.x_peers[1:] + here.y_peers[1:] + [here.twin])
     theirs = 2 * (1 - c)
     swaps = [
@@ -279,7 +319,7 @@
         copy.wait()
 
 
-def gather_first(qkv, out, up, down, lens, mixing, tokens, cot, earlier, vecs, count, batches, outer, inner, ident):
+def gather_first(qkv, out, up, down, lens, mixing, tokens, cot, earlier, vecs, batches, outer, inner, ident):
     across = inner // 2
     share = qkv.shape[0]
     tall = tokens.shape[0]
@@ -294,12 +334,12 @@
             jax.ShapeDtypeStruct((4,) + grid + (2 * share, D), bf16),
             jax.ShapeDtypeStruct((2, outer, 2 * share, D), bf16),
             jax.ShapeDtypeStruct((outer, BLOCKS * share, D), bf16),
-            jax.ShapeDtypeStruct((batches,) + count.shape, count.dtype),
+            jax.ShapeDtypeStruct((batches, 8, 128), jnp.int32),
             jax.ShapeDtypeStruct((tall, D), bf16),
             jax.ShapeDtypeStruct((tall, D), f32),
             jax.ShapeDtypeStruct((16, D), f32),
         ),
-        in_specs=[IN_VMEM] * 4 + [IN_SMEM] * 2 + [IN_VMEM] * 2 + [ANYWHERE, IN_VMEM, ANYWHERE],
+        in_specs=[IN_VMEM] * 4 + [IN_SMEM] * 2 + [IN_VMEM] * 2 + [ANYWHERE, IN_VMEM],
         out_specs=(ANYWHERE,) * 4 + (IN_VMEM,) * 3,
         scratch_shapes=[
             pltpu.VMEM((8, share, D), f32),
@@ -308,6 +348,7 @@
             pltpu.VMEM((2, 2 * share, D), bf16),
             pltpu.VMEM((BLOCKS * share, D), bf16),
             pltpu.VMEM((2, tall, D), bf16),
+            pltpu.VMEM((8, 128), jnp.int32),
         ]
         + [DMA((outer, 2))] * 2
         + [DMA((2, outer, across, batches))] * 6
@@ -317,7 +358,7 @@
         + [DMA((5,)), DMA((earlier.shape[0],))],
         compiler_params=remote_params(ident, ROOM),
         name="gather_first",
-    )(qkv, out, up, down, lens, mixing, tokens, cot, earlier, vecs, count)
+    )(qkv, out, up, down, lens, mixing, tokens, cot, earlier, vecs)
 
 
 def spread_kernel(batches, outer, inner, with_rest, *refs):
@@ -447,32 +488,6 @@
     )(normed, near, vecs, cosine, sine, *lines)
 
 
-def swap_kernel(batches, inner, x, out, send, recv, local):
-    outer = x.shape[0]
-    here = Place(batches, outer, inner)
-    greet(here.z_peers[1:])
-    own = carry(x.at[here.o], out.at[here.o], local)
-    copies = []
-    for t in range(1, outer):
-        copies.append(push(x.at[here.zs[t]], out.at[here.o], send.at[t], recv.at[t], here.z_peers[t]))
-    own.wait()
-    for copy in copies:
-        copy.wait()
-
-
-def swap_outer(x, batches, inner, ident):
-    outer = x.shape[0]
-    return pl.pallas_call(
-        functools.partial(swap_kernel, batches, inner),
-        out_shape=jax.ShapeDtypeStruct(x.shape, x.dtype),
-        in_specs=[ANYWHERE],
-        out_specs=ANYWHERE,
-        scratch_shapes=[DMA((outer,)), DMA((outer,)), DMA],
-        compiler_params=remote_params(ident),
-        name="swap_heads",
-    )(x)
-
-
 def half_rows(block_t, half):
     z = jnp.zeros((HEAD, block_t.shape[1]), block_t.dtype)
     if half == 0:
@@ -555,9 +570,11 @@
                 total_exp = l_s[h : h + 1]
                 ot[z, span_u, :] = ot[z, span_u, :] / total_exp
                 lse[z, u : u + 1, :] = m_s[h : h + 1] + jnp.log(total_exp)
-        for t in range(width // 128):
-            lanes = slice(128 * t, 128 * t + 128)
-            o[z, :, lanes] = ot[z, lanes, :].T.astype(bf16)
+        for g in range(groups):
+            pair, single = HEAD * UNITS[g][0], HEAD * UNITS[g][2]
+            o[z, g, :rows, :] = ot[z, pair : pair + 128, :].T.astype(bf16)
+            halves = [ot[z, single : single + HEAD, : rows // 2], ot[z, single : single + HEAD, rows // 2 :]]
+            o[z, g, rows:, :] = jnp.concatenate(halves, 0).T.astype(bf16)
         return 0
 
     lax.fori_loop(0, outer, one, 0)
@@ -571,7 +588,7 @@
     return pl.pallas_call(
         functools.partial(attend_kernel, groups, per, span, inner),
         out_shape=(
-            jax.ShapeDtypeStruct((outer, rows, width), bf16),
+            jax.ShapeDtypeStruct((outer, groups, rows + rows // 2, 128), bf16),
             jax.ShapeDtypeStruct((outer, width, rows), f32),
             jax.ShapeDtypeStruct((outer, 8, rows), f32),
         ),
@@ -612,18 +629,31 @@
         for t in range(width // 128):
             lanes = slice(128 * t, 128 * t + 128)
             small = (q[z, :, lanes] * 0.125).astype(bf16)
-            grad = do[z, :, lanes]
             turned = small.T
-            grad_t = grad.T
-            prod = grad_t.astype(f32) * ot[z, lanes, :]
             for half in range(2):
                 u = 2 * t + half
                 qt[u] = half_rows(turned, half)
-                dot_t[u] = half_rows(grad_t, half)
                 keep = low if half == 0 else ~low
                 qz[u] = jnp.where(keep, small, jnp.zeros_like(small))
-                dz[u] = jnp.where(keep, grad, jnp.zeros_like(grad))
-                rd[u : u + 1, :] = jnp.sum(prod[HEAD * half : HEAD * half + HEAD], 0, keepdims=True)
+        for g in range(groups):
+            pair = do[z, g, :rows, :]
+            single = do[z, g, rows:, :]
+            pair_t, single_t = pair.T, single.T
+            single_t = jnp.concatenate([single_t[:HEAD], single_t[HEAD:]], 1)
+            blank = jnp.zeros_like(single_t)
+            wide = unfold_single(single.astype(f32), g == 1)
+            for half in range(2):
+                u = UNITS[g][half]
+                dot_t[u] = half_rows(pair_t, half)
+                dz[u] = jnp.where(low if half == 0 else ~low, pair, jnp.zeros_like(pair))
+            u = UNITS[g][2]
+            dot_t[u] = jnp.concatenate([single_t, blank] if g == 0 else [blank, single_t], 0)
+            dz[u] = jnp.where(low if g == 0 else ~low, wide, 0.0).astype(bf16)
+            for h in range(per):
+                u = UNITS[g][h]
+                span_u = slice(HEAD * u, HEAD * u + HEAD)
+                grad_t = single_t if h == 2 else pair_t[HEAD * h : HEAD * h + HEAD]
+                rd[u : u + 1, :] = jnp.sum(grad_t.astype(f32) * ot[z, span_u, :], 0, keepdims=True)
         dqt[...] = jnp.zeros(dqt.shape, f32)
         for g in range(groups):
             length = lens[g]
@@ -716,105 +746,159 @@
     )(lens, q, k, v, do, ot, lse, cos, sin)
 
 
-def middle_kernel(outer, home, tokens, cot, mixture, dots, near, up, down, vecs, lens, mixing, total, mixed, sent, middle_grad, out_term, up_terms, down_terms, sums, attended, middle, hat_s, low_s, low_t, result_s, acc, back, weights, sems):
+def middle_kernel(batches, outer, inner, *refs):
+    refs = list(refs)
+
+    def take(n):
+        got = refs[:n]
+        del refs[:n]
+        return got
+
+    o_mine, near, up, down, tokens, cot, mixture, counts, vecs, lens, mixing = take(11)
+    mixed, grad_mine, middle_grad, out_term, up_terms, down_terms, sums = take(7)
+    home, sent, attended, middle, low_s, result_s, slope_s, active_s, hidden_s, acc, back, weights = take(12)
+    fetch, hs, hr, gs, gr, local = refs
     tall = tokens.shape[0]
     groups = lens.shape[0]
     rows = tall // groups
-    fetch_out = carry(near.at[3], weights.at[0], sems.at[0])
-    fetch_up = carry(up, weights.at[pl.ds(1, BLOCKS)], sems.at[1])
-    fetch_down = carry(down, weights.at[pl.ds(1 + BLOCKS, BLOCKS)], sems.at[2])
+    here = Place(batches, outer, inner)
+    o = here.o
+    fetches = [
+        carry(down, weights.at[pl.ds(1 + BLOCKS, BLOCKS)], fetch.at[0]),
+        carry(near.at[3], weights.at[0], fetch.at[1]),
+        carry(up, weights.at[pl.ds(1, BLOCKS)], fetch.at[2]),
+    ]
+    greet(here.z_peers[1:])
+    coming, waits = {}, []
     for g in range(groups):
-        tiles = take_heads(lambda o, t: home[o, :, 128 * t : 128 * t + 128].astype(f32), g, outer)
+        coming[g] = [carry(o_mine.at[o, g], home.at[o, g], local.at[0, g])]
+        for t in range(1, outer):
+            coming[g].append(push(o_mine.at[here.zs[t], g], home.at[o, g], hs.at[g, t], hr.at[g, t], here.z_peers[t]))
+    count = counts[0, 0:1, 0:1]
+    for y in range(1, batches):
+        count = count + counts[y, 0:1, 0:1]
+    slots = lax.axis_size("batch") * lax.axis_size("seq") * tall
+    scale = slots / count.astype(f32)
+    row = lax.broadcasted_iota(jnp.int32, (rows, 1), 0) + lax.axis_index("seq") * rows
+
+    def grad_of(g):
+        return cot[g * rows : g * rows + rows, :].astype(f32) * jnp.where(row < lens[g], scale, 0.0)
+
+    sums[...] = jnp.zeros(sums.shape, f32)
+    for g in range(groups):
+        here_rows = slice(g * rows, g * rows + rows)
+        result = (mixing[0] * grad_of(g)).astype(bf16)
+        result_s[here_rows] = result
+        sums[8 + BLOCKS : 9 + BLOCKS] = sums[8 + BLOCKS : 9 + BLOCKS] + jnp.sum(result.astype(f32), 0, keepdims=True)
+    fetches[0].wait()
+
+    def early(i, _):
+        slope_s[i] = mm_nt(result_s[...], weights[1 + BLOCKS + i])
+        return 0
+
+    lax.fori_loop(0, BLOCKS, early, 0)
+    for g in range(groups):
+        here_rows = slice(g * rows, g * rows + rows)
+        for copy in coming[g]:
+            copy.wait()
+        tiles = unfold_heads(lambda p: home[p, g].astype(f32), rows, outer)
         for i, tile in enumerate(tiles):
-            attended[g * rows : g * rows + rows, 128 * i : 128 * i + 128] = tile.astype(bf16)
-    fetch_out.wait()
-    value = tokens[...].astype(f32) + (mm(attended[...], weights[0]) + vecs[7:8])
-    middle[...] = value
-    hat, inverse = normalize(value)
-    hat_s[...] = hat
-    low = (hat * vecs[1:2] + vecs[3:4]).astype(bf16)
-    low_s[...] = low
-    low_t[...] = low.T
-    slots = lax.axis_size("batch") * lax.axis_size("seq") * tall
-    scale = slots / total[0].astype(f32)
-    row = lax.broadcasted_iota(jnp.int32, (rows, 1), 0) + lax.axis_index("seq") * rows
-    live = jnp.concatenate([jnp.where(row < lens[g], scale, 0.0) for g in range(groups)], 0)
-    grad = cot[...].astype(f32) * live
-    result = (mixing[0] * grad).astype(bf16)
-    result_s[...] = result
-    sums[...] = jnp.zeros(sums.shape, f32)
-    sums[8 + BLOCKS : 9 + BLOCKS] = jnp.sum(result.astype(f32), 0, keepdims=True)
-    acc[...] = jnp.zeros(acc.shape, f32)
-    back[...] = jnp.zeros(back.shape, f32)
-    fetch_up.wait()
-    fetch_down.wait()
-
-    def block(i, _):
-        up_i = weights[1 + i]
-        down_i = weights[1 + BLOCKS + i]
-        hidden = mm(low_s[...], up_i) + vecs[pl.ds(8 + i, 1)]
-        square = hidden * hidden
-        bend = jnp.tanh(0.7978845608028654 * (hidden + 0.044715 * square * hidden))
-        half = 0.5 * (1.0 + bend)
-        active = (hidden * half).astype(bf16)
-        slope = half + 0.5 * hidden * (1.0 - bend * bend) * (0.7978845608028654 * (1.0 + 3.0 * 0.044715 * square))
-        acc[...] += mm(active, down_i)
-        down_terms[i] = mm(active.T, result_s[...]).astype(bf16)
-        hidden_grad = (slope * mm_nt(result_s[...], down_i)).astype(bf16)
-        sums[pl.ds(8 + i, 1)] = jnp.sum(hidden_grad.astype(f32), 0, keepdims=True)
-        up_terms[i] = mm(low_t[...], hidden_grad).astype(bf16)
-        back[...] += mm_nt(hidden_grad, up_i)
+            attended[here_rows, 128 * i : 128 * i + 128] = tile.astype(bf16)
+        if g == 0:
+            fetches[1].wait()
+        value = tokens[here_rows].astype(f32) + (mm(attended[here_rows], weights[0]) + vecs[7:8])
+        middle[here_rows] = value
+        hat, inverse = normalize(value)
+        low_s[here_rows] = (hat * vecs[1:2] + vecs[3:4]).astype(bf16)
+        acc[here_rows] = jnp.zeros((rows, D), f32)
+        back[...] = jnp.zeros((rows, D), f32)
+        if g == 0:
+            fetches[2].wait()
+
+        def block(i, _):
+            hidden = mm(low_s[here_rows], weights[1 + i]) + vecs[pl.ds(8 + i, 1)]
+            square = hidden * hidden
+            bend = jnp.tanh(0.7978845608028654 * (hidden + 0.044715 * square * hidden))
+            half = 0.5 * (1.0 + bend)
+            active = (hidden * half).astype(bf16)
+            active_s[i, here_rows] = active
+            slope = half + 0.5 * hidden * (1.0 - bend * bend) * (0.7978845608028654 * (1.0 + 3.0 * 0.044715 * square))
+            hidden_grad = (slope * slope_s[i, here_rows]).astype(bf16)
+            hidden_s[i, here_rows] = hidden_grad
+            sums[pl.ds(8 + i, 1)] = sums[pl.ds(8 + i, 1)] + jnp.sum(hidden_grad.astype(f32), 0, keepdims=True)
+            back[...] += mm_nt(hidden_grad, weights[1 + i])
+            acc[here_rows] += mm(active, weights[1 + BLOCKS + i])
+            return 0
+
+        lax.fori_loop(0, BLOCKS, block, 0)
+        inner_grad = back[...]
+        sums[1:2] = sums[1:2] + jnp.sum(inner_grad * hat, 0, keepdims=True)
+        sums[3:4] = sums[3:4] + jnp.sum(inner_grad, 0, keepdims=True)
+        total_grad = mixing[0] * grad_of(g) + normalize_back(inner_grad, hat, inverse, vecs[1:2])
+        middle_grad[here_rows] = total_grad
+        branch = total_grad.astype(bf16)
+        sums[7:8] = sums[7:8] + jnp.sum(branch.astype(f32), 0, keepdims=True)
+        back[...] = mm_nt(branch, weights[0])
+
+        def write(target, value):
+            sent[target, g] = value.astype(bf16)
+
+        fold_heads_of(write, lambda t: back[:, 128 * t : 128 * t + 128], outer)
+        for t in range(1, outer):
+            waits.append(push(sent.at[here.zs[t], g], grad_mine.at[o, g], gs.at[g, t], gr.at[g, t], here.z_peers[t]))
+        waits.append(carry(sent.at[o, g], grad_mine.at[o, g], local.at[1, g]))
+
+    low_t = low_s[...].T
+
+    def late(i, _):
+        down_terms[i] = mm(active_s[i].T, result_s[...]).astype(bf16)
+        up_terms[i] = mm(low_t, hidden_s[i]).astype(bf16)
         return 0
 
-    lax.fori_loop(0, BLOCKS, block, 0)
-    layer_out = middle[...] + acc[...] + vecs[8 + BLOCKS : 9 + BLOCKS]
-    mixed[...] = (mixture[...] + mixing[0] * layer_out).astype(bf16)
-    grad = cot[...].astype(f32) * live
-    sums[VECTORS : VECTORS + 1] = jnp.sum(grad * layer_out, 0, keepdims=True)
-    hat = hat_s[...]
-    inner_grad = back[...]
-    sums[1:2] = jnp.sum(inner_grad * hat, 0, keepdims=True)
-    sums[3:4] = jnp.sum(inner_grad, 0, keepdims=True)
-    total_grad = mixing[0] * grad + normalize_back(inner_grad, hat, inverse, vecs[1:2])
-    middle_grad[...] = total_grad
-    branch = total_grad.astype(bf16)
-    sums[7:8] = jnp.sum(branch.astype(f32), 0, keepdims=True)
-    out_term[...] = mm(attended[...].T, branch).astype(bf16)
-    acc[...] = mm_nt(branch, weights[0])
-
-    def write(target, tile, value):
-        sent[target, :, 128 * tile : 128 * tile + 128] = value.astype(bf16)
-
-    put_heads(write, lambda g, t: acc[g * rows : g * rows + rows, 128 * t : 128 * t + 128], outer)
-
-
-def middle_layer(home, tokens, cot, mixture, dots, near, up, down, vecs, lens, mixing, total, outer):
+    lax.fori_loop(0, BLOCKS, late, 0)
+    out_term[...] = mm(attended[...].T, middle_grad[...].astype(bf16)).astype(bf16)
+    for g in range(groups):
+        here_rows = slice(g * rows, g * rows + rows)
+        layer_out = middle[here_rows] + acc[here_rows] + vecs[8 + BLOCKS : 9 + BLOCKS]
+        mixed[here_rows] = (mixture[here_rows] + mixing[0] * layer_out).astype(bf16)
+        sums[VECTORS : VECTORS + 1] = sums[VECTORS : VECTORS + 1] + jnp.sum(grad_of(g) * layer_out, 0, keepdims=True)
+    for copy in waits:
+        copy.wait()
+
+
+def middle_layer(o_mine, near, up, down, tokens, cot, mixture, counts, vecs, lens, mixing, batches, outer, inner, ident):
     tall = tokens.shape[0]
+    groups = lens.shape[0]
     wide = pltpu.VMEM((tall, D), f32)
     low = pltpu.VMEM((tall, D), bf16)
+    hidden = pltpu.VMEM((BLOCKS, tall, D), bf16)
     return pl.pallas_call(
-        functools.partial(middle_kernel, outer),
+        functools.partial(middle_kernel, batches, outer, inner),
         out_shape=(
             jax.ShapeDtypeStruct((tall, D), bf16),
-            jax.ShapeDtypeStruct(home.shape, bf16),
+            jax.ShapeDtypeStruct(o_mine.shape, bf16),
             jax.ShapeDtypeStruct((tall, D), f32),
             jax.ShapeDtypeStruct((D, D), bf16),
             jax.ShapeDtypeStruct((BLOCKS, D, D), bf16),
             jax.ShapeDtypeStruct((BLOCKS, D, D), bf16),
             jax.ShapeDtypeStruct((16, D), f32),
         ),
-        in_specs=[IN_VMEM] * 5 + [ANYWHERE] * 3 + [IN_VMEM] + [IN_SMEM] * 3,
-        out_specs=(IN_VMEM,) * 7,
+        in_specs=[ANYWHERE] * 4 + [IN_VMEM] * 5 + [IN_SMEM] * 2,
+        out_specs=(IN_VMEM, ANYWHERE) + (IN_VMEM,) * 5,
         scratch_shapes=[
-            low, wide, wide, low, pltpu.VMEM((D, tall), bf16), low, wide, wide,
+            pltpu.VMEM(o_mine.shape, bf16), pltpu.VMEM(o_mine.shape, bf16),
+            low, wide, low, low, pltpu.VMEM((BLOCKS, tall, D), f32), hidden, hidden,
+            wide, pltpu.VMEM((tall // groups, D), f32),
             pltpu.VMEM((1 + 2 * BLOCKS, D, D), bf16), DMA((3,)),
-        ],
-        compiler_params=params(),
+        ]
+        + [DMA((groups, outer))] * 4
+        + [DMA((2, groups))],
+        compiler_params=remote_params(ident, ROOM),
         name="middle_layer",
-    )(home, tokens, cot, mixture, dots, near, up, down, vecs, lens, mixing, total)
-
-
-def back_kernel(outer, dq, dk, dv, cosine, sine, normed, tokens, near, vecs, cot, lens, mixing, total, middle_grad, out_term, sums, dots, input_grad, terms, small, joined, low_t):
+    )(o_mine, near, up, down, tokens, cot, mixture, counts, vecs, lens, mixing)
+
+
+def back_kernel(outer, dq, dk, dv, cosine, sine, normed, tokens, near, vecs, cot, counts, lens, mixing, middle_grad, out_term, sums, dots, input_grad, terms, small, joined, low_t):
     tall = tokens.shape[0]
     groups = lens.shape[0]
     rows = tall // groups
@@ -838,7 +922,10 @@
     small[0:1] = jnp.sum(back * hat, 0, keepdims=True)
     small[2:3] = jnp.sum(back, 0, keepdims=True)
     slots = lax.axis_size("batch") * lax.axis_size("seq") * tall
-    scale = slots / total[0].astype(f32)
+    count = counts[0, 0:1, 0:1]
+    for y in range(1, counts.shape[0]):
+        count = count + counts[y, 0:1, 0:1]
+    scale = slots / count.astype(f32)
     row = lax.broadcasted_iota(jnp.int32, (rows, 1), 0) + lax.axis_index("seq") * rows
     live = jnp.concatenate([jnp.where(row < lens[g], scale, 0.0) for g in range(groups)], 0)
     grad = cot[...].astype(f32) * live
@@ -850,7 +937,7 @@
     small[VECTORS : VECTORS + 1] = line
 
 
-def back_layer(dq, dk, dv, cosine, sine, normed, tokens, near, vecs, cot, lens, mixing, total, middle_grad, out_term, sums, dots, outer):
+def back_layer(dq, dk, dv, cosine, sine, normed, tokens, near, vecs, cot, counts, lens, mixing, middle_grad, out_term, sums, dots, outer):
     tall = tokens.shape[0]
     return pl.pallas_call(
         functools.partial(back_kernel, outer),
@@ -859,12 +946,12 @@
             jax.ShapeDtypeStruct((4, D, D), bf16),
             jax.ShapeDtypeStruct((16, D), f32),
         ),
-        in_specs=[IN_VMEM] * 10 + [IN_SMEM] * 3 + [IN_VMEM] * 4,
+        in_specs=[IN_VMEM] * 11 + [IN_SMEM] * 2 + [IN_VMEM] * 4,
         out_specs=(IN_VMEM,) * 3,
         scratch_shapes=[pltpu.VMEM((3, tall, D), bf16), pltpu.VMEM((D, tall), bf16)],
         compiler_params=params(),
         name="back_layer",
-    )(dq, dk, dv, cosine, sine, normed, tokens, near, vecs, cot, lens, mixing, total, middle_grad, out_term, sums, dots)
+    )(dq, dk, dv, cosine, sine, normed, tokens, near, vecs, cot, counts, lens, mixing, middle_grad, out_term, sums, dots)
 
 
 def adam(param, grad, first, second, decay):
@@ -1289,7 +1376,6 @@
     earlier = earlier_outs.reshape(-1, tall, D)
     vecs = jnp.pad(small_params[: VECTORS * D].reshape(VECTORS, D), ((0, 16 - VECTORS), (0, 0)))
     mixing = small_params[VECTORS * D :]
-    mine = jnp.sum(seq_lengths)
 
     freq = 10000.0 ** (-jnp.arange(HEAD // 2, dtype=f32) * 2.0 / HEAD)
     query_pos = seq_rank * rows + jnp.arange(rows, dtype=jnp.int32)
@@ -1310,17 +1396,16 @@
     if remote:
         near, up_line, down_line, counts, normed, mixture, dots = gather_first(
             qkv_weight, out_weight, up_weight, down_weight, seq_lengths, mixing, tokens, cot, earlier, vecs,
-            jnp.full((8, 128), mine, jnp.int32), batches, outer, inner, 1,
+            batches, outer, inner, 1,
         )
         near = near.reshape(4, D, D)
-        total = jnp.sum(counts[:, 0, 0]).reshape(1)
         q, k, v, up, down = spread_heads(normed, near, vecs, cosine, sine, (up_line, down_line), batches, outer, inner, 2)
         up, down = up.reshape(BLOCKS, D, D), down.reshape(BLOCKS, D, D)
     else:
         near = by_blocks(lax.all_gather(jnp.concatenate([by_rows(qkv_weight), by_rows(out_weight)], 0), everywhere, axis=0))
         up = by_blocks(lax.all_gather(by_rows(up_weight), everywhere, axis=0))
         down = lax.all_gather(down_weight.astype(bf16), everywhere, axis=0).reshape(BLOCKS, D, D)
-        total = lax.psum(mine, "batch").reshape(1)
+        counts = jnp.full((1, 8, 128), lax.psum(jnp.sum(seq_lengths), "batch"), jnp.int32)
         wide = tokens.astype(f32)
         normed = (normalize(wide)[0] * vecs[0] + vecs[2]).astype(bf16)
         live = (query_pos[None, :] < seq_lengths[:, None]).astype(f32).reshape(tall, 1)
@@ -1332,11 +1417,9 @@
 
     k, v = k.reshape(length, width), v.reshape(length, width)
     attended, turned_out, log_total = attend(seq_lengths, q, k, v, groups, per, inner, math.gcd(length, 1024))
-    home = swap_outer(attended, batches, inner, 3)
-    mixed, sent, middle_grad, out_term, up_terms, down_terms, sums = middle_layer(
-        home, tokens, cot, mixture, dots, near, up, down, vecs, seq_lengths, mixing, total, outer
+    mixed, grad_mine, middle_grad, out_term, up_terms, down_terms, sums = middle_layer(
+        attended, near, up, down, tokens, cot, mixture, counts, vecs, seq_lengths, mixing, batches, outer, inner, 3
     )
-    grad_mine = swap_outer(sent, batches, inner, 4)
     dq, dk, dv = attend_back(
         seq_lengths, q, k, v, grad_mine, turned_out, log_total, block_cos, block_sin, groups, per, inner, math.gcd(length, 512)
     )
@@ -1348,7 +1431,7 @@
     else:
         dq, dk, dv = fold_heads(dq, dk, dv, (), batches, inner, 5)
     input_grad, near_terms, small = back_layer(
-        dq, dk, dv, cosine, sine, normed, tokens, near, vecs, cot, seq_lengths, mixing, total, middle_grad, out_term, sums, dots, outer
+        dq, dk, dv, cosine, sine, normed, tokens, near, vecs, cot, counts, seq_lengths, mixing, middle_grad, out_term, sums, dots, outer
     )
     if remote:
         near_grad, up_grad, down_grad, small = reduce_last(

time: 422 us -> 393 us (0.931); the launches traced: 414 us -> 393 us
  Pallas kernels: 402 us -> 385 us
    pallas_call x3 -> x1, Pallas kernels: 68.1 us -> 45.7 us  [middle_layer(): pl.pallas_call(functools.partial(middle_kernel, batches, outer, inner), o...]
    pallas_call x1, Pallas kernels: 82.5 us -> 94.1 us  [fold_heads(): pl.pallas_call(functools.partial(fold_kernel, batches, inner, with_rest),...]
where the time goes in v1:
time: 393 us
  Pallas kernels  385 us (98%)
    pallas_call x1, Pallas kernels, fold_heads(): pl.pallas_call(functools.partial(fold_kernel, batches, inner, with_rest),...  94.1 us
    pallas_call x1, Pallas kernels, spread_heads(): pl.pallas_call(functools.partial(spread_kernel, batches, outer, inner, wi...  71.5 us
    pallas_call x1, Pallas kernels, gather_first(): pl.pallas_call(functools.partial(first_kernel, batches, outer, inner, fir...  52 us
    pallas_call x1, Pallas kernels, reduce_last(): pl.pallas_call(functools.partial(last_kernel, batches, outer, inner), out...  50.4 us
    pallas_call x1, Pallas kernels, middle_layer(): pl.pallas_call(functools.partial(middle_kernel, batches, outer, inner), o...  45.7 us
    pallas_call x1, Pallas kernels, attend_back(): pl.pallas_call(functools.partial(attend_back_kernel, groups, per, span, i...  29.1 us
    pallas_call x1, Pallas kernels, attend(): pl.pallas_call(functools.partial(attend_kernel, groups, per, span, inner)...  26.1 us
    pallas_call x1, Pallas kernels, back_layer(): pl.pallas_call(functools.partial(back_kernel, outer), out_shape=(jax.Shap...  12.2 us

profile of v1, /device:TPU:0, one launch (start us, length us, event | category | flops | bytes accessed | tf_op | source)
XLA Modules:
  0.0 393.3 jit_solution(18069571457740710592)
XLA Ops:
  0.7 0.5 fusion
  1.2 1.0 pad_maximum_fusion
  2.2 0.8 reshape.130
  3.0 0.6 pad.4.refs_9_.refs_2_.refs_8_.vecs
  3.6 1.2 slice.9.refs_5_.refs_10_.mixing
  4.8 52.0 %gather_first.1 = (bf16[4,2,4,2,48,768]{5,4,3,2,1,0:T(8,128)(2,1)}, bf16[2,4,48,768]{3,2,1,0:T(8,128)(2,1)}, bf16[4,96,768]{2,1,0:T(8,128)(2,1)}, s32[2,8,128]{2...) custom-call(f32[24,2304]{1,0:T(8,128)} %refs_0_.3, f32[24,768]{1,0:T(8,128)} %refs_3_.3, ...), custom_call_target="tpu_custom_call" | custom-call | tf_op jit(solution)/shard_map/gather_first/pallas_call | solution.py:331
  56.8 71.5 %spread_heads.1 = (bf16[4,256,384]{2,1,0:T(8,128)(2,1)}, bf16[4,4,256,384]{3,2,1,0:T(8,128)(2,1)}, bf16[4,4,256,384]{3,2,1,0:T(8,128)(2,1)}, bf16[4,2,4,2,48,768...) custom-call(bf16[512,768]{1,0:T(8,128)(2,1)} %get-tuple-element.66.refs_0_.normed, bf16[4,768,768]{2,1,0:T(8,128)(2,1)} %bitcast.16, ...), custom_call_target="tpu_custom_call" | custom-call | tf_op jit(solution)/shard_map/spread_heads/pallas_call | solution.py:480
  128.3 26.1 %attend.1 = (bf16[4,2,384,128]{3,2,1,0:T(8,128)(2,1)}, f32[4,384,256]{2,1,0:T(8,128)}, f32[4,8,256]{2,1,0:T(8,128)}) custom-call(s32[2]{0:T(128)} %lens.5, bf16[4,256,384]{2,1,0:T(8,128)(2,1)} %get-tuple-element.70.q, bf16[4096,384]{1,0:T(8,128)(2,1)} %bitcast.19, bf16[4096,384]{1,0:T(8,128)(2,1)} %bitcast.21), custom_call_target="tpu_custom_call" | custom-call | tf_op jit(solution)/shard_map/attend/pallas_call | solution.py:588
  154.4 45.7 %middle_layer.1 = (bf16[512,768]{1,0:T(8,128)(2,1)}, bf16[4,2,384,128]{3,2,1,0:T(8,128)(2,1)}, f32[512,768]{1,0:T(8,128)}, bf16[768,768]{1,0:T(8,128)(2,1)}, bf1...) custom-call(bf16[4,2,384,128]{3,2,1,0:T(8,128)(2,1)} %get-tuple-element.73.refs_0_, ...), custom_call_target="tpu_custom_call" | custom-call | tf_op jit(solution)/shard_map/middle_layer/pallas_call | solution.py:875
  200.1 0.1 add_convert_fusion
  200.2 1.2 multiply_sine_fusion
  201.5 29.1 %attend_back.1 = (bf16[4,256,384]{2,1,0:T(8,128)(2,1)}, bf16[4096,384]{1,0:T(8,128)(2,1)}, bf16[4096,384]{1,0:T(8,128)(2,1)}) custom-call(s32[2]{0:T(128)} %lens.5, bf16[4,256,384]{2,1,0:T(8,128)(2,1)} %get-tuple-element.70.q, bf16[4096,384]{1,0:T(8,128)(2,1)} %bitcast.20, bf16[4096,384]{1,0:T(8,128)(2,1)} %bitcast.22, ...), custom_call_target="tpu_custom_call" | custom-call | tf_op jit(solution)/shard_map/attend_back/pallas_call | solution.py:724
  230.6 94.1 %fold_heads.1 = (bf16[4,256,384]{2,1,0:T(8,128)(2,1)}, bf16[4,256,384]{2,1,0:T(8,128)(2,1)}, bf16[4,256,384]{2,1,0:T(8,128)(2,1)}, bf16[2,4,48,768]{3,2,1,0:T(8,128)(2,1)}, bf16[4,96,768]{2,1,0:T(8,128)(2,1)}) custom-call(bf16[4,256,384]{2,1,0:T(8,128)(2,1)} %get-tuple-element.82.refs_0_, bf16[4,4,256,384]{3,2,1,0:T(8,128)(2,1)} %bitcast.35, ...), custom_call_target="tpu_custom_call" | custom-call | tf_op jit(solution)/shard_map/fold_heads/pallas_call | solution.py:1158
  324.7 12.2 %back_layer.1 = (f32[512,768]{1,0:T(8,128)}, bf16[4,768,768]{2,1,0:T(8,128)(2,1)}, f32[16,768]{1,0:T(8,128)}) custom-call(bf16[4,256,384]{2,1,0:T(8,128)(2,1)} %get-tuple-element.87.dq, bf16[4,256,384]{2,1,0:T(8,128)(2,1)} %get-tuple-element.88.dk, bf16[4,256,384]{2,1,0:T(8,128)(2,1)} %get-tuple-element.89.dv, f32[256,128]{1,0:T(8,128)} %get-tuple-element.123.refs_3_.cosine, ...), custom_call_target="tpu_custom_call" | custom-call | tf_op jit(solution)/shard_map/back_layer/pallas_call | solution.py:942
  336.9 50.4 %reduce_last.1 = (f32[4,24,768]{2,1,0:T(8,128)}, f32[4,24,768]{2,1,0:T(8,128)}, f32[96,768]{1,0:T(8,128)}, f32[16,768]{1,0:T(8,128)}) custom-call(bf16[4,2,4,2,48,768]{5,4,3,2,1,0:T(8,128)(2,1)} %bitcast.32, bf16[2,4,48,768]{3,2,1,0:T(8,128)(2,1)} %get-tuple-element.96.refs_1_, bf16[4,96,768]{2,1,0:T(8,128)(2,1)} %get-tuple-element.97.refs_2_, ...), custom_call_target="tpu_custom_call" | custom-call | tf_op jit(solution)/shard_map/reduce_last/pallas_call | solution.py:1321
  387.4 0.0 copy-start.1
  387.4 0.0 copy-start.3
  387.4 0.0 copy-start.4
  387.4 3.8 adam_all.1
  391.2 0.0 copy-done.2
  391.2 0.0 copy-done.1
  391.2 0.0 copy-done.3
  391.3 0.7 fusion.7
  391.9 0.9 copy.38
  (8 shorter events, 0.0 us)
Async XLA Ops:
  387.4 3.9 copy-start.2
  387.4 3.9 copy-start.1
  387.4 3.9 copy-start.3
  387.4 3.9 copy-start.4
  387.4 4.5 %copy-start = (bf16[512,768]{1,0:T(8,128)(2,1)S(1)}, bf16[512,768]{1,0:T(8,128)(2,1)}, u32[]{:S(2)}) copy-start(bf16[512,768]{1,0:T(8,128)(2,1)} %get-tuple-element.78) | copy-start | bytes 2359300
